TPU v7x, 32 devices: a whole 2x2x4 slice. The times are simulated.
32 devices in a mesh: dp: 4 (over y, x), tensor: 4 (over z), layers: 2 (over core).
Axes of the slice: x: 2, y: 2, z: 4, core: 2. Of those that a mesh axis runs over, the one named last changes fastest.
Arguments:
- section_input: bfloat16 [2, 512, 4096], P('layers', 'dp', 'tensor'), may hold values from -24 to 24
- out_cotangent: bfloat16 [512, 4096], P('dp', 'tensor'), may hold values from -24 to 24
- lift_weight: bfloat16 [2, 2048, 4096], P('layers', None, 'tensor'), may hold values from -0.125 to 0.125
- proj_weight: bfloat16 [2, 4096, 4096], P('layers', None, 'tensor'), may hold values from -0.09375 to 0.09375
- lift_mask: int32 [2, 16, 32], P('layers', None, 'tensor'), may hold values 0 or 1
- proj_mask: int32 [2, 32, 32], P('layers', None, 'tensor'), may hold values 0 or 1
- channel_perm: int32 [2, 4096], P('layers'), may hold values from 0 to 4095, each once within a row
- lift_moment: float32 [2, 2048, 4096], P('layers', 'dp', 'tensor'), may hold values from -3 to 3
- lift_square: float32 [2, 2048, 4096], P('layers', 'dp', 'tensor'), may hold values from 0.25 to 1
- proj_moment: float32 [2, 4096, 4096], P('layers', 'dp', 'tensor'), may hold values from -3 to 3
- proj_square: float32 [2, 4096, 4096], P('layers', 'dp', 'tensor'), may hold values from 0.25 to 1
Outputs:
- input_grad: float32 [2, 512, 4096], P('layers', 'dp', 'tensor')
- log_det: float32 [2], P('layers')
- lift_first: float32 [2, 2048, 4096], P('layers', 'dp', 'tensor')
- lift_second: float32 [2, 2048, 4096], P('layers', 'dp', 'tensor')
- lift_update: float32 [2, 2048, 4096], P('layers', 'dp', 'tensor')
- proj_first: float32 [2, 4096, 4096], P('layers', 'dp', 'tensor')
- proj_second: float32 [2, 4096, 4096], P('layers', 'dp', 'tensor')
- proj_update: float32 [2, 4096, 4096], P('layers', 'dp', 'tensor')
Inputs may be any that keep to these rules, and one draw needn't show every extreme that they name: `channel_perm`: each row orders all 4096 features once. `lift_mask`: 1 keeps a block of 128 x 128 weights, 0 prunes it. `proj_mask`: 1 keeps a block of 128 x 128 weights, 0 prunes it.
All inputs are finite; a program needn't handle non-finite values.
Results may differ from a plain program's by a relative error of at most 0.008.
Values may be sent and summed in bfloat16 or wider, within the bound.
No kernel may reach another device: no remote copies, remote signals or barrier semaphores. Data moves between devices by JAX's collectives and lax.ppermute only.
A program may use at most 128 MiB of HBM per device.

v0:
```python
import jax
import jax.numpy as jnp
from jax import lax
from jax.sharding import PartitionSpec as P

BLK = 128
ADAM_STEP = 10
CLIP = 4096


beta_one = 0.9
beta_two = 0.99
adam_eps = 1e-08


def passed_along(block, axis, distance):
    devices = range(lax.axis_size(axis))
    route = [(i - distance, i) for i in devices if i - distance in devices]
    return lax.ppermute(block, axis, route)


def expand_blocks(block_mask):
    blk_rows, blk_cols = block_mask.shape
    widened = jnp.broadcast_to((block_mask > 0)[:, None, :, None], (blk_rows, BLK, blk_cols, BLK))
    return widened.reshape(blk_rows * BLK, blk_cols * BLK)


def contract_rows(left_mat, right_mat):
    return lax.dot_general(
        left_mat, right_mat, (((0,), (0,)), ((), ())), preferred_element_type=jnp.float32
    )


def contract_cols(left_mat, right_mat):
    return lax.dot_general(
        left_mat, right_mat, (((1,), (1,)), ((), ())), preferred_element_type=jnp.float32
    )


def adam_step(gradient, kept, moment, square, factor):
    scaled = gradient * factor
    new_first = jnp.where(kept, beta_one * moment + (1.0 - beta_one) * scaled, moment)
    new_second = jnp.where(kept, beta_two * square + (1.0 - beta_two) * scaled * scaled, square)
    bias_one = 1.0 - beta_one**ADAM_STEP
    bias_two = 1.0 - beta_two**ADAM_STEP
    update = jnp.where(
        kept, new_first / bias_one / (jnp.sqrt(new_second / bias_two) + adam_eps), 0.0
    )
    return (new_first[None], new_second[None], update[None])


def per_device(
    section_input,
    out_cotangent,
    lift_weight,
    proj_weight,
    lift_mask,
    proj_mask,
    channel_perm,
    lift_moment,
    lift_square,
    proj_moment,
    proj_square,
):
    section_idx = lax.axis_index("layers")
    dp_size = lax.axis_size("dp")
    dp_index = lax.axis_index("dp")
    tensor_size = lax.axis_size("tensor")
    tensor_index = lax.axis_index("tensor")
    tokens, gathered_cot = (
        lax.all_gather(section_input[0], "tensor", axis=1, tiled=True),
        lax.all_gather(out_cotangent, "tensor", axis=1, tiled=True),
    )
    channel_order = channel_perm[0]
    feat_width = channel_order.shape[0]
    half_width = feat_width // 2
    tok_rows = tokens.shape[0]
    lift_keep = expand_blocks(lift_mask[0])
    proj_keep = expand_blocks(proj_mask[0])
    lift_eff = jnp.where(lift_keep, lift_weight[0], jnp.zeros((), jnp.bfloat16))
    proj_eff = jnp.where(proj_keep, proj_weight[0], jnp.zeros((), jnp.bfloat16))
    permuted = jnp.take(tokens, channel_order, axis=1)
    cond_side = permuted[:, :half_width]
    moved_side = permuted[:, half_width:].astype(jnp.float32)
    pre_act = jnp.dot(cond_side, lift_eff, preferred_element_type=jnp.float32)
    hidden = jax.nn.silu(pre_act).astype(jnp.bfloat16)
    shared = lax.psum(contract_cols(hidden, proj_eff).astype(jnp.bfloat16), "tensor").astype(
        jnp.float32
    )
    raw_scale = shared[:, :half_width]
    shift_term = shared[:, half_width:]
    scale_term = jax.nn.sigmoid(raw_scale + 2.0)
    keep_part = 1.0 - scale_term
    squash = jax.nn.sigmoid(pre_act)
    silu_slope = squash * (1.0 + pre_act * (1.0 - squash))
    inverse = (
        jnp.zeros((feat_width,), jnp.int32)
        .at[channel_order]
        .set(jnp.arange(feat_width, dtype=jnp.int32))
    )
    own_cols = half_width // tensor_size
    own_raw = lax.dynamic_slice_in_dim(raw_scale, tensor_index * own_cols, own_cols, 1)
    log_part = jnp.sum(jax.nn.log_sigmoid(own_raw + 2.0))
    log_total = lax.psum(log_part, ("dp", "tensor"))

    def backward(grad_out):
        grad_cond = grad_out[:, :half_width]
        grad_moved = grad_out[:, half_width:]
        grad_raw = grad_moved * (moved_side + shift_term) * scale_term * keep_part - keep_part
        grad_shift = grad_moved * scale_term
        grad_st = jnp.concatenate([grad_raw, grad_shift], axis=1).astype(jnp.bfloat16)
        grad_act = jnp.dot(grad_st, proj_eff, preferred_element_type=jnp.float32)
        grad_pre = (grad_act * silu_slope).astype(jnp.bfloat16)
        grad_inputs = grad_cond + lax.psum(
            contract_cols(grad_pre, lift_eff).astype(jnp.bfloat16), "tensor"
        ).astype(jnp.float32)
        grad_mixed = jnp.concatenate([grad_inputs, grad_shift], axis=1)
        return (grad_mixed, grad_st, grad_pre)

    incoming = gathered_cot.astype(jnp.float32)
    early_mixed = backward(incoming)[0]
    early_grad = jnp.take(early_mixed, inverse, axis=1)
    passed = passed_along(early_grad.astype(jnp.bfloat16), "layers", -1)
    arriving = jnp.where(section_idx == 0, passed.astype(jnp.float32), incoming)
    grad_mixed, grad_st, grad_pre = backward(arriving)
    lift_rows = lift_moment.shape[1]
    proj_rows = proj_moment.shape[1]
    cond_cols, st_cols = (
        lax.all_to_all(cond_side, "dp", split_axis=1, concat_axis=0, tiled=True),
        lax.all_to_all(grad_st, "dp", split_axis=1, concat_axis=0, tiled=True),
    )
    lift_grad = contract_rows(cond_cols, lax.all_gather(grad_pre, "dp", axis=0, tiled=True))
    proj_grad = contract_rows(st_cols, lax.all_gather(hidden, "dp", axis=0, tiled=True))
    lift_own = lax.dynamic_slice_in_dim(lift_keep, dp_index * lift_rows, lift_rows, 0)
    proj_own = lax.dynamic_slice_in_dim(proj_keep, dp_index * proj_rows, proj_rows, 0)
    lift_grad = jnp.where(lift_own, lift_grad, 0.0)
    proj_grad = jnp.where(proj_own, proj_grad, 0.0)
    local_sq = jnp.sum(lift_grad * lift_grad) + jnp.sum(proj_grad * proj_grad)
    square_total = lax.psum(local_sq, ("dp", "tensor", "layers"))
    factor = jnp.minimum(1.0, CLIP / (jnp.sqrt(square_total) + 1e-06))
    lift_out = adam_step(lift_grad, lift_own, lift_moment[0], lift_square[0], factor)
    proj_out = adam_step(proj_grad, proj_own, proj_moment[0], proj_square[0], factor)
    grad_cols = feat_width // tensor_size
    own_inverse = lax.dynamic_slice_in_dim(inverse, tensor_index * grad_cols, grad_cols, 0)
    input_grad = jnp.take(grad_mixed, own_inverse, axis=1)[None]
    log_det = (log_total / (tok_rows * dp_size * half_width)).reshape(1)
    return (
        input_grad,
        log_det,
        lift_out[0],
        lift_out[1],
        lift_out[2],
        proj_out[0],
        proj_out[1],
        proj_out[2],
    )


def solution(mesh):
    return jax.shard_map(
        per_device,
        mesh=mesh,
        in_specs=(
            P("layers", "dp", "tensor"),
            P("dp", "tensor"),
            P("layers", None, "tensor"),
            P("layers", None, "tensor"),
            P("layers", None, "tensor"),
            P("layers", None, "tensor"),
            P("layers", None),
            P("layers", "dp", "tensor"),
            P("layers", "dp", "tensor"),
            P("layers", "dp", "tensor"),
            P("layers", "dp", "tensor"),
        ),
        out_specs=(
            P("layers", "dp", "tensor"),
            P("layers"),
            P("layers", "dp", "tensor"),
            P("layers", "dp", "tensor"),
            P("layers", "dp", "tensor"),
            P("layers", "dp", "tensor"),
            P("layers", "dp", "tensor"),
            P("layers", "dp", "tensor"),
        ),
        check_vma=False,
    )
```

profile of v0, /device:TPU:0, one launch (start us, length us, event | category | flops | bytes accessed | tf_op | source)
XLA Modules:
  0.0 399.0 jit_solution(7298965249447110378)
XLA Ops:
  12.9 27.9 %all-gather.12.cloned.1.call-done = bf16[1,128,4096]{1,2,0:T(8,128)(2,1)} async-done(((bf16[1,128,1024]{1,2,0:T(8,128)(2,1)}), bf16[1,128,4096]{1,2,0:T(8,128)(2,1)}) %all-gather.12.cloned.1.call-update) | async-done | bytes 1048592 | tf_op jit(solution)/shard_map/all_gather | solution.py:71
  40.8 12.4 %gather_fusion = bf16[4096,128]{1,0:T(8,128)(2,1)S(1)} fusion(bf16[128,4096]{0,1:T(8,128)(2,1)} %bitcast.146, s32[4096]{0:T(1024)S(1)} %broadcast_clamp_fusion), kind=kCustom, calls=%fused_computation | custom fusion | bytes 2113536 | tf_op jit(solution)/shard_map/jit(_take)/gather | solution.py:82
  62.6 7.7 %convolution_convert_fusion = bf16[128,4096]{1,0:T(8,128)(2,1)} fusion(bf16[128,1024]{1,0:T(8,128)(2,1)S(1)} %get-tuple-element.33, bf16[1,4096,1024]{2,1,0:T(8,128)(2,1)} %param.14, pred[512,8,8,128]{3,2,1,0:T(8,128)(4,1)S(1)} %bitcast.147), kind=kOutput, calls=%fused_computation.8 | convolution fusion | flops 1078460416 | bytes 13893632 | tf_op jit(solution)/shard_map/dot_general | solution.py:35
  70.6 2.8 convert_element_type.42
  73.4 50.7 %all-reduce.4.cloned.1.call-done = bf16[128,4096]{1,0:T(8,128)(2,1)} async-done(((bf16[128,4096]{1,0:T(8,128)(2,1)}), bf16[128,4096]{1,0:T(8,128)(2,1)}) %all-reduce.4.cloned.1.call-update) | async-done | bytes 1048592 | tf_op jit(solution)/shard_map/psum | solution.py:87
  129.3 12.4 %convolution_convert_fusion.2 = bf16[128,2048]{1,0:T(8,128)(2,1)} fusion(bf16[1,2048,1024]{2,1,0:T(8,128)(2,1)} %param.13, bf16[1,4096,1024]{2,1,0:T(8,128)(2,1)} %param.14, bf16[128,2048]{1,0:T(8,128)(2,1)} %slice_multiply_fusion.1, bf16[128,2048]{1,0:T(8,128)(2,1)} %fusion.13, f32[128,1024]{1,0:T(8,128)} %get-tuple-element.34, ...), kind=kOutput, calls=%fused_computation.20 | convolution fusion | flops 1620443136 | bytes 20971520 | tf_op jit(solution)/shard_map/dot_general | solution.py:35
  141.7 15.5 %scatter_custom_fusion = s32[4096]{0:T(1024)S(1)} fusion(s32[4096]{0:T(1024)S(1)} %bitcast.165, s32[4096]{0:T(1024)S(1)} %iota.3, s32[]{:T(128)} %constant.31.clone.1), kind=kCustom, calls=%fused_computation.80 | custom fusion | bytes 16388 | tf_op jit(solution)/shard_map/scatter | solution.py:99
  157.3 22.2 %all-reduce.6.cloned.1.call-done = bf16[128,2048]{1,0:T(8,128)(2,1)} async-done(((bf16[128,2048]{1,0:T(8,128)(2,1)}), bf16[128,2048]{1,0:T(8,128)(2,1)}) %all-reduce.6.cloned.1.call-update) | async-done | bytes 524304 | tf_op jit(solution)/shard_map/psum | solution.py:114
  183.6 15.0 %gather_fusion.1 = bf16[4096,128]{1,0:T(8,128)(2,1)} fusion(bf16[128,4096]{0,1:T(8,128)(2,1)S(1)} %copy.31, s32[4096]{0:T(1024)S(1)} %fusion.27), kind=kCustom, calls=%fused_computation.1 | custom fusion | bytes 2113536 | tf_op jit(solution)/shard_map/jit(_take)/gather | solution.py:122
  205.0 3.3 collective-permute-done
  212.8 6.6 %fusion.10 = bf16[128,1024]{1,0:T(8,128)(2,1)S(1)} fusion(bf16[1,4096,1024]{2,1,0:T(8,128)(2,1)} %param.14, bf16[128,2048]{1,0:T(8,128)(2,1)S(1)} %get-tuple-element.24, bf16[128,2048]{1,0:T(8,128)(2,1)S(1)} %get-tuple-element.32, f32[128,1024]{1,0:T(8,128)S(1)} %copy-done.22, pred[512,8,8,128]{3,2,1,0:T(8,128)(4,1)S(1)} %bitcast.149), kind=kOutput, calls=%fused_computation.41 | convolution fusion | flops 1081212928 | bytes 14417920 | tf_op jit(solution)/shard_map/dot_general | solution.py:112
  219.4 4.8 %convolution_convert_fusion.1 = bf16[128,2048]{1,0:T(8,128)(2,1)} fusion(bf16[128,1024]{1,0:T(8,128)(2,1)S(1)} %fusion.10, bf16[1,2048,1024]{2,1,0:T(8,128)(2,1)} %param.13, pred[256,8,8,128]{3,2,1,0:T(8,128)(4,1)S(1)} %bitcast.153), kind=kOutput, calls=%fused_computation.19 | convolution fusion | flops 539230208 | bytes 7077888 | tf_op jit(solution)/shard_map/dot_general | solution.py:35
  227.5 4.1 %copy.69 = pred[512,8,8,128]{3,1,2,0:T(8,128)(4,1)} copy(pred[512,8,8,128]{3,2,1,0:T(8,128)(4,1)S(1)} %bitcast.150) | data formatting | bytes 8388608
  235.8 41.7 %psum.38 = f32[]{:T(128)} all-reduce(f32[]{:T(128)S(6)} %neg.25), channel_id=1, replica_groups=mesh['dp'=4,'tensor'=4,'layers'=2] {'dp','tensor'}, use_global_device_ids=true, to_apply=%region_5.6 | all-reduce | flops 1 | bytes 8 | tf_op jit(solution)/shard_map/psum | solution.py:104
  280.6 4.2 %all-to-all-start.1 = ((bf16[128,4,1024]{2,0,1:T(8,128)(2,1)}), bf16[128,4,1024]{2,0,1:T(8,128)(2,1)}, u32[]{:S(2)}, u32[]{:S(2)}) async-start(bf16[128,4,1024]{2,0,1:T(8,128)(2,1)} %pad_maximum_fusion.2), calls=%async_computation.1 | async-start | bytes 2097152 | tf_op jit(solution)/shard_map/all_to_all | solution.py:130
  289.5 2.8 gather_fusion.2
  292.5 10.1 %all-to-all-done.1 = bf16[128,4,1024]{2,0,1:T(8,128)(2,1)} async-done(((bf16[128,4,1024]{2,0,1:T(8,128)(2,1)}), bf16[128,4,1024]{2,0,1:T(8,128)(2,1)}, u32[]{:S(2)}, u32[]{:S(2)}) %all-to-all-start.1) | async-done | bytes 1048608 | tf_op jit(solution)/shard_map/all_to_all | solution.py:130
  302.6 3.7 all-to-all-start
  306.3 6.0 %multiply_reduce_fusion = (f32[]{:T(128)}, f32[1024,1024]{1,0:T(8,128)}) fusion(bf16[512,1024]{1,0:T(8,128)(2,1)} %bitcast.17, bf16[512,1024]{1,0:T(8,128)(2,1)} %all-gather.10.cloned.1.call-done, pred[4096,1024]{1,0:T(8,128)(4,1)} %bitcast.155, s32[]{:T(128)S(6)} %select_n.122), kind=kOutput, calls=%fused_computation.17 | convolution fusion | flops 1076887552 | bytes 7340040 | tf_op jit(solution)/shard_map/dot_general | solution.py:29
  313.5 15.1 %all-gather.8.cloned.1.call-done = bf16[512,1024]{1,0:T(8,128)(2,1)} async-done(((bf16[128,1024]{1,0:T(8,128)(2,1)}), bf16[512,1024]{1,0:T(8,128)(2,1)}) %all-gather.8.cloned.1.call-update) | async-done | bytes 1048592 | tf_op jit(solution)/shard_map/all_gather | solution.py:132
  328.7 3.9 multiply_reduce_fusion.1
  334.8 39.3 %psum.39 = f32[]{:T(128)} all-reduce(f32[]{:T(128)S(6)} %add.149), channel_id=1, replica_groups=mesh['dp'=4,'tensor'=4,'layers'=2] {'dp','tensor','layers'}, use_global_device_ids=true, to_apply=%region_8.9 | all-reduce | flops 1 | bytes 8 | tf_op jit(solution)/shard_map/psum | solution.py:139
  374.9 7.3 %select_bitcast_fusion.1 = (f32[1,512,1024]{2,1,0:T(8,128)}, f32[1,512,1024]{2,1,0:T(8,128)}, f32[1,512,1024]{2,1,0:T(8,128)}) fusion(pred[2048,1024]{1,0:T(8,128)(4,1)S(1)} %bitcast.158, s32[]{:T(128)S(6)} %select_n.120, f32[512,1024]{1,0:T(8,128)} %get-tuple-element.36, f32[]{:T(128)S(6)} %min.3, f32[1,512,1024]{2,1,0:T(8,128)} %param.18, ...), kind=kLoop, calls=%fused_computation.33 | loop fusion | flops 7864320 | bytes 13107208 | tf_op jit(solution)/shard_map/broadcast_in_dim | solution.py:49
  383.6 7.5 %select_bitcast_fusion = (f32[1,1024,1024]{2,1,0:T(8,128)}, f32[1,1024,1024]{2,1,0:T(8,128)}, f32[1,1024,1024]{2,1,0:T(8,128)}) fusion(pred[4096,1024]{1,0:T(8,128)(4,1)} %bitcast.156, s32[]{:T(128)S(6)} %select_n.122, f32[1024,1024]{1,0:T(8,128)S(1)} %copy-done.12, f32[]{:T(128)S(6)} %min.3, f32[1,1024,1024]{2,1,0:T(8,128)S(1)} %copy-done.10, ...), kind=kLoop, calls=%fused_computation.16 | loop fusion | flops 15728640 | bytes 26214408 | tf_op jit(solution)/shard_map/broadcast_in_dim | solution.py:49
  (105 shorter events, 53.0 us)
Async XLA Ops:
  7.2 33.6 %all-gather.12.cloned.1.call-start = ((), (), s32[]{:S(2)}) async-start(), calls=%async_computation.8 | async-start | bytes 1310720 | tf_op jit(solution)/shard_map/all_gather | solution.py:71
  9.0 61.6 %all-gather.6.cloned.1.call-start = ((), (), s32[]{:S(2)}) async-start(), calls=%async_computation.2 | async-start | bytes 1310720 | tf_op jit(solution)/shard_map/all_gather | solution.py:72
  9.8 114.4 %all-reduce.4.cloned.1.call-start = ((), (), s32[]{:S(2)}) async-start(), calls=%async_computation.3 | async-start | bytes 2097152 | tf_op jit(solution)/shard_map/psum | solution.py:87
  53.9 74.1 %copy-start.8 = (bf16[128,4096]{1,0:T(8,128)(2,1)}, bf16[128,4096]{1,0:T(8,128)(2,1)S(1)}, u32[]{:S(2)}) copy-start(bf16[128,4096]{1,0:T(8,128)(2,1)S(1)} %select_bitcast_fusion.2) | copy-start | bytes 3145732
  54.5 5.0 %copy-start.4 = (pred[16,128,8,128]{3,2,1,0:T(8,128)(4,1)}, pred[16,128,8,128]{3,2,1,0:T(8,128)(4,1)S(1)}, u32[]{:S(2)}) copy-start(pred[16,128,8,128]{3,2,1,0:T(8,128)(4,1)S(1)} %broadcast_in_dim.88) | copy-start | bytes 6291460
  59.5 10.9 %copy-start.19 = (bf16[128,1024]{1,0:T(8,128)(2,1)}, bf16[128,1024]{1,0:T(8,128)(2,1)S(1)}, u32[]{:S(2)}) copy-start(bf16[128,1024]{1,0:T(8,128)(2,1)S(1)} %get-tuple-element.33) | copy-start | bytes 786436
  70.4 109.1 %all-reduce.6.cloned.1.call-start = ((), (), s32[]{:S(2)}) async-start(), calls=%async_computation.4 | async-start | bytes 1048576 | tf_op jit(solution)/shard_map/psum | solution.py:114
  129.3 51.7 %copy-start.16 = (bf16[128,2048]{1,0:T(8,128)(2,1)S(1)}, bf16[128,2048]{1,0:T(8,128)(2,1)}, u32[]{:S(2)}) copy-start(bf16[128,2048]{1,0:T(8,128)(2,1)} %slice_multiply_fusion.1) | copy-start | bytes 1572868
  141.7 143.2 %all-reduce.8.cloned.1.call-start = ((), (), s32[]{:S(2)}) async-start(), calls=%async_computation.5 | async-start | bytes 1048576 | tf_op jit(solution)/shard_map/psum | solution.py:114
  198.7 11.4 %copy-start.9 = (bf16[128,4096]{1,0:T(8,128)(2,1)S(1)}, bf16[128,4096]{1,0:T(8,128)(2,1)}, u32[]{:S(2)}) copy-start(bf16[128,4096]{1,0:T(8,128)(2,1)} %copy-done.8) | copy-start | bytes 3145732
  203.4 4.9 %collective-permute-start = (bf16[128,4096]{1,0:T(8,128)(2,1)}, bf16[128,4096]{1,0:T(8,128)(2,1)}, u32[]{:S(2)}, u32[]{:S(2)}) collective-permute-start(bf16[128,4096]{1,0:T(8,128)(2,1)} %fusion.15), channel_id=1, source_target_pairs={{1,0},{3,2},{5,4},{7,6},{9,8},{11,10},{13,12},{15,14},{17,16},{19,... | collective-permute-start | bytes 3145736 | tf_op jit(solution)/shard_map/ppermute | solution.py:19
  204.9 7.8 %copy-start.1 = (pred[32,128,8,128]{3,2,1,0:T(8,128)(4,1)S(1)}, pred[32,128,8,128]{3,2,1,0:T(8,128)(4,1)}, u32[]{:S(2)}) copy-start(pred[32,128,8,128]{3,2,1,0:T(8,128)(4,1)} %copy-done) | copy-start | bytes 12582916
  204.9 7.8 %copy-start.22 = (f32[128,1024]{1,0:T(8,128)S(1)}, f32[128,1024]{1,0:T(8,128)}, u32[]{:S(2)}) copy-start(f32[128,1024]{1,0:T(8,128)} %get-tuple-element.34) | copy-start | bytes 1572868
  212.8 6.6 %copy-start.5 = (pred[16,128,8,128]{3,2,1,0:T(8,128)(4,1)S(1)}, pred[16,128,8,128]{3,2,1,0:T(8,128)(4,1)}, u32[]{:S(2)}) copy-start(pred[16,128,8,128]{3,2,1,0:T(8,128)(4,1)} %copy-done.4) | copy-start | bytes 6291460
  224.2 82.1 %all-gather.10.cloned.1.call-start = ((), (), s32[]{:S(2)}) async-start(), calls=%async_computation.7 | async-start | bytes 1310720 | tf_op jit(solution)/shard_map/all_gather | solution.py:133
  224.8 103.9 %all-gather.8.cloned.1.call-start = ((), (), s32[]{:S(2)}) async-start(), calls=%async_computation.6 | async-start | bytes 1310720 | tf_op jit(solution)/shard_map/all_gather | solution.py:132
  232.5 52.4 %copy-start.7 = (f32[128,4096]{1,0:T(8,128)S(1)}, f32[128,4096]{1,0:T(8,128)}, u32[]{:S(2)}) copy-start(f32[128,4096]{1,0:T(8,128)} %copy-done.6) | copy-start | bytes 6291460
  278.2 7.9 %copy-start.14 = (f32[128,2048]{1,0:T(8,128)S(1)}, f32[128,2048]{1,0:T(8,128)}, u32[]{:S(2)}) copy-start(f32[128,2048]{1,0:T(8,128)} %get-tuple-element.25) | copy-start | bytes 3145732
  280.6 21.9 %all-to-all-start.1 = ((bf16[128,4,1024]{2,0,1:T(8,128)(2,1)}), bf16[128,4,1024]{2,0,1:T(8,128)(2,1)}, u32[]{:S(2)}, u32[]{:S(2)}) async-start(bf16[128,4,1024]{2,0,1:T(8,128)(2,1)} %pad_maximum_fusion.2), calls=%async_computation.1 | async-start | bytes 2097152 | tf_op jit(solution)/shard_map/all_to_all | solution.py:130
  302.6 11.0 %all-to-all-start = ((bf16[128,4,512]{2,0,1:T(8,128)(2,1)}), bf16[128,4,512]{2,0,1:T(8,128)(2,1)S(1)}, u32[]{:S(2)}, u32[]{:S(2)}) async-start(bf16[128,4,512]{2,0,1:T(8,128)(2,1)} %bitcast.144), calls=%async_computation | async-start | bytes 1048576 | tf_op jit(solution)/shard_map/all_to_all | solution.py:129
  306.3 22.3 %copy-start.15 = (pred[256,8,8,128]{3,1,2,0:T(8,128)(4,1)S(1)}, pred[256,8,8,128]{3,1,2,0:T(8,128)(4,1)}, u32[]{:S(2)}) copy-start(pred[256,8,8,128]{3,1,2,0:T(8,128)(4,1)} %copy.70) | copy-start | bytes 6291460
  374.8 7.3 %copy-start.10 = (f32[1,1024,1024]{2,1,0:T(8,128)S(1)}, f32[1,1024,1024]{2,1,0:T(8,128)}, u32[]{:S(2)}) copy-start(f32[1,1024,1024]{2,1,0:T(8,128)} %param.20) | copy-start | bytes 12582916
  374.9 7.3 %copy-start.11 = (f32[1,1024,1024]{2,1,0:T(8,128)S(1)}, f32[1,1024,1024]{2,1,0:T(8,128)}, u32[]{:S(2)}) copy-start(f32[1,1024,1024]{2,1,0:T(8,128)} %param.21) | copy-start | bytes 12582916
  374.9 8.7 %copy-start.12 = (f32[1024,1024]{1,0:T(8,128)S(1)}, f32[1024,1024]{1,0:T(8,128)}, u32[]{:S(2)}) copy-start(f32[1024,1024]{1,0:T(8,128)} %get-tuple-element.38) | copy-start | bytes 12582916
  (9 other events, 25.0 us)
Sparse Core Ops, SparseCore 0:
  10.1 30.6 all-gather.11
  42.4 27.4 all-gather.5
  72.8 51.3 all-reduce.3
  141.8 37.6 all-reduce.5
  224.3 38.3 all-reduce.7
  264.5 38.1 all-gather.9
  304.8 23.8 all-gather.7
where the time goes:
time: 400 us; the launch traced here: 399 us
  waiting for transfers between devices  132 us (33%)
  blocking collectives  80.9 us (20%)
  local copies, waits for them, and re-layouts  74.8 us (19%)
  matrix products  43.8 us (11%)
  other arithmetic  38.6 us (10%)
  between operations  19 us (5%)
  starting transfers between devices  9.94 us (2%)
    psum x1, waiting for transfers between devices, per_device(): lax.psum(contract_cols(hidden, proj_eff).astype(jnp.bfloat16), 'tensor')  50.7 us
    psum x1, blocking collectives, per_device(): log_total = lax.psum(log_part, ('dp', 'tensor'))  41.7 us
    psum x1, blocking collectives, per_device(): square_total = lax.psum(local_sq, ('dp', 'tensor', 'layers'))  39.3 us
    all_gather x1, waiting for transfers between devices, per_device(): lax.all_gather(section_input[0], 'tensor', axis=1, tiled=True)  27.9 us
    dot_general x3, matrix products, contract_cols(): lax.dot_general(left_mat, right_mat, (((1,), (1,)), ((), ())), preferred_...  24.8 us
    psum x2, waiting for transfers between devices, backward(): lax.psum(contract_cols(grad_pre, lift_eff).astype(jnp.bfloat16), 'tensor')  22.2 us
    gather x2, local copies, waits for them, and re-layouts, per_device(): early_grad = jnp.take(early_mixed, inverse, axis=1)  17.4 us
    unnamed x50, local copies, waits for them, and re-layouts  16.6 us
  transfers between devices with their start and end apart: 10, of which 7 were waited for; matrix products, arithmetic and copies ran while one was open for 18% of the time, Pallas kernels for 0%

commit v1 on v0

v1 whole, which is shorter than its diff:
```python
import jax
import jax.numpy as jnp
from jax import lax
from jax.experimental import pallas as pl
from jax.experimental.pallas import tpu as pltpu
from jax.sharding import PartitionSpec as P

BLK = 128
ADAM_STEP = 10
CLIP = 4096

beta_one = 0.9
beta_two = 0.99
adam_eps = 1e-08

BF = jnp.bfloat16
F32 = jnp.float32
VMEM_LIMIT = 16 * 1024 * 1024


def vspec():
    return pl.BlockSpec(memory_space=pltpu.VMEM)


def sspec():
    return pl.BlockSpec(memory_space=pltpu.SMEM)


def params():
    return pltpu.CompilerParams(vmem_limit_bytes=VMEM_LIMIT)


def dot_nn(a, b):
    return lax.dot_general(a, b, (((1,), (0,)), ((), ())), preferred_element_type=F32)


def dot_nt(a, b):
    return lax.dot_general(a, b, (((1,), (1,)), ((), ())), preferred_element_type=F32)


def dot_tn(a, b):
    return lax.dot_general(a, b, (((0,), (0,)), ((), ())), preferred_element_type=F32)


def sigmoid(x):
    return 1.0 / (1.0 + jnp.exp(-x))


def xor_pairs(n, k):
    return [(i, i ^ k) for i in range(n)]


def over_tensor(x, pairs, layer):
    n_layers = lax.axis_size("layers")
    layers = range(n_layers) if layer is None else (layer,)
    route = [(a * n_layers + s, b * n_layers + s) for a, b in pairs for s in layers]
    return lax.ppermute(x, ("tensor", "layers"), route)


def over_dp(x, pairs, layer):
    n_layers = lax.axis_size("layers")
    layers = range(n_layers) if layer is None else (layer,)
    route = [(a * n_layers + s, b * n_layers + s) for a, b in pairs for s in layers]
    return lax.ppermute(x, ("dp", "layers"), route)


def scatter_tensor(chunks, layer):
    n = lax.axis_size("tensor")
    got = {k: over_tensor(chunks[k], xor_pairs(n, k), layer) for k in far_first(n)}
    return [chunks[0]] + [got[k] for k in range(1, n)]


def gather_tensor(x, layer):
    return scatter_tensor([x] * lax.axis_size("tensor"), layer)


def far_first(n):
    return sorted(range(1, n), key=lambda k: k < n // 2)


def scatter_dp(chunks, layer):
    n = lax.axis_size("dp")
    got = {k: over_dp(chunks[k], xor_pairs(n, k), layer) for k in reversed(range(1, n))}
    return [chunks[0]] + [got[k] for k in range(1, n)]


def down_a_section(chunks):
    n = lax.axis_size("tensor")
    m = lax.axis_size("layers")
    got = {
        k: lax.ppermute(
            chunks[k], ("tensor", "layers"), [(i * m + 1, j * m) for i, j in xor_pairs(n, k)]
        )
        for k in far_first(n)
    }
    got[0] = lax.ppermute(chunks[0], "layers", [(1, 0)])
    return [got[k] for k in range(n)]


def spread_halves(low, high, tensor_index):
    n = lax.axis_size("tensor")
    early = tensor_index < n // 2
    one = over_tensor(
        jnp.where(early, low, high),
        [(i, 2 * i if i < n // 2 else 2 * i + 1 - n) for i in range(n)],
        1,
    )
    two = over_tensor(
        jnp.where(early, high, low),
        [(i, 2 * i + 1 if i < n // 2 else 2 * i - n) for i in range(n)],
        1,
    )
    even = tensor_index % 2 == 0
    return jnp.where(even, one, two), jnp.where(even, two, one)


def whole(body, name, ins, outs, scratch=(), deps=()):
    arrays = [in_hbm(x) if m == pltpu.HBM else x for x, m in ins]
    specs = [pl.BlockSpec(memory_space=m) for _, m in ins]
    n_in, n_dep = len(arrays), len(deps)

    def run(*refs):
        body(*refs[:n_in], *refs[n_in + n_dep :])

    return pl.pallas_call(
        run,
        in_specs=specs + [pl.BlockSpec(memory_space=pl.ANY)] * n_dep,
        out_specs=[vspec()] * len(outs),
        out_shape=[jax.ShapeDtypeStruct(s, d) for s, d in outs],
        scratch_shapes=list(scratch),
        compiler_params=params(),
        name=name,
    )(*arrays, *deps)


def on_vmem(arrays):
    return [(x, pltpu.VMEM) for x in arrays]


def in_hbm(x):
    return pltpu.with_memory_space_constraint(x, pltpu.HBM)


def tile_width(width):
    return next(c for c in (512, 256, 128) if width % c == 0)


def tiles_of(width):
    tile = tile_width(width)
    return [slice(i, i + tile) for i in range(0, width, tile)]


def loads(src, dst, sems, count):
    rows = src.shape[0] // count
    return [
        pltpu.make_async_copy(
            src.at[pl.ds(c * rows, rows)], dst.at[pl.ds(c * rows, rows)], sems.at[c]
        )
        for c in range(count)
    ]


SPAN = 256


def span_of(size):
    return next(c for c in (SPAN, SPAN // 2) if size % c == 0)


def fill_hot(hot_s, at, row, base, span):
    width = row.shape[1]
    near = jnp.broadcast_to(row - base, (16, width)).astype(BF)
    step = lax.broadcasted_iota(jnp.int32, (16, width), 0).astype(F32)
    for i in range(0, span, 16):
        hit = (step + float(i)).astype(BF) == near
        hot_s[at + i : at + i + 16, :] = jnp.where(
            hit, jnp.ones((16, width), BF), jnp.zeros((16, width), BF)
        )


def prep_weights(lift_mask, proj_mask, lift, proj):
    steps = min(8, lift.shape[0] // BLK)

    def body(lift_mask_ref, proj_mask_ref, lift_ref, proj_ref, lift_out, proj_out):
        for mask, src, dst in (
            (lift_mask_ref, lift_ref, lift_out),
            (proj_mask_ref, proj_ref, proj_out),
        ):
            n_rows = src.shape[0] // BLK
            for r in range(n_rows):
                for c in range(src.shape[1] // BLK):
                    at = (slice(r * BLK, (r + 1) * BLK), slice(c * BLK, (c + 1) * BLK))
                    kept = mask[pl.program_id(0) * n_rows + r, c] > 0
                    tile = src[at]
                    dst[at] = jnp.where(kept, tile, jnp.zeros_like(tile))

    specs = [
        pl.BlockSpec((x.shape[0] // steps, x.shape[1]), lambda i: (i, 0)) for x in (lift, proj)
    ]
    return pl.pallas_call(
        body,
        grid=(steps,),
        in_specs=[sspec(), sspec()] + specs,
        out_specs=specs,
        out_shape=[pltpu.HBM(lift.shape, BF), pltpu.HBM(proj.shape, BF)],
        compiler_params=params(),
        name="prep_weights",
    )(lift_mask, proj_mask, in_hbm(lift), in_hbm(proj))


def prep_inverse(perm, feat, deps):
    width = perm.shape[1]
    tile = tile_width(width)
    span = span_of(feat)

    def body(perm_ref, inv_ref, hot_s):
        lane = lax.broadcasted_iota(jnp.int32, (16, tile), 1)
        which = lax.broadcasted_iota(jnp.int32, (16, tile), 0)

        def step(s, _):
            base = s * span
            acc = jnp.zeros((16, span), F32)
            for c in range(width // tile):
                fill_hot(
                    hot_s, 0, perm_ref[:, c * tile : (c + 1) * tile], base.astype(F32), span
                )
                place = lane + (c * tile + 1)
                value = jnp.where(which == 0, place // 64, jnp.where(which == 1, place % 64, 0))
                acc = acc + dot_nt(value.astype(F32).astype(BF), hot_s[...])
            inv = acc[0:1, :] * 64.0 + acc[1:2, :] - 1.0
            inv_ref[:, pl.ds(pl.multiple_of(base, span), span)] = inv
            return 0

        lax.fori_loop(0, feat // span, step, 0)

    return whole(
        body,
        "prep_inverse",
        on_vmem([perm]),
        [((1, feat), F32)],
        [pltpu.VMEM((span, tile), BF)],
        deps=deps,
    )[0]


def forward(idx, tokens, perm, lift, proj, n, deps):
    rows, block = tokens[0].shape
    width = perm.shape[1]
    half, hid = lift.shape
    hb = half // n
    tile = tile_width(width)
    span = span_of(block)

    def body(idx_ref, *refs):
        tok = refs[:n]
        perm_ref, lift_h, proj_h, slope_ref, perm_s, hidden_ref = refs[n : n + 6]
        shared_out = refs[n + 6 : n + 6 + n]
        hot_s, lift_ref, proj_ref, lift_sem, proj_sem = refs[-5:]
        t = idx_ref[0]
        lift_in = loads(lift_h, lift_ref, lift_sem, n)
        proj_in = loads(proj_h, proj_ref, proj_sem, 2 * n)
        for copy in lift_in + proj_in:
            copy.start()

        def columns(c, _):
            cols = pl.ds(pl.multiple_of(c * tile, tile), tile)
            row = perm_ref[:, cols]
            acc = jnp.zeros((rows, tile), F32)
            for k in range(n):
                for i in range(0, block, span):
                    base = ((t ^ k) * block + i).astype(F32)
                    fill_hot(hot_s.at[k % 2], i, row, base, span)
                acc = acc + dot_nn(tok[k][...], hot_s[k % 2])
            perm_s[:, cols] = acc.astype(BF)
            return 0

        lax.fori_loop(0, width // tile, columns, 0)
        for copy in lift_in:
            copy.wait()
        for cols in tiles_of(hid):
            pre = dot_nn(perm_s[:, :half], lift_ref[:, cols])
            squash = sigmoid(pre)
            hidden_ref[:, cols] = (pre * squash).astype(BF)
            slope_ref[:, cols] = squash * (1.0 + pre * (1.0 - squash))
        hidden = hidden_ref[...]
        for copy in proj_in:
            copy.wait()
        for k in range(n):
            at = pl.multiple_of((t ^ k) * hb, hb)
            shared_out[k][:, :hb] = dot_nt(hidden, proj_ref[pl.ds(at, hb), :]).astype(BF)
            shared_out[k][:, hb:] = dot_nt(hidden, proj_ref[pl.ds(half + at, hb), :]).astype(BF)

    outs = whole(
        body,
        "forward",
        [(idx, pltpu.SMEM)]
        + on_vmem(list(tokens) + [perm])
        + [(lift, pltpu.HBM), (proj, pltpu.HBM)],
        [((rows, hid), F32), ((rows, width), BF), ((rows, hid), BF)]
        + [((rows, 2 * hb), BF)] * n,
        [
            pltpu.VMEM((2, block, tile), BF),
            pltpu.VMEM(lift.shape, BF),
            pltpu.VMEM(proj.shape, BF),
            pltpu.SemaphoreType.DMA((n,)),
            pltpu.SemaphoreType.DMA((2 * n,)),
        ],
        deps=deps,
    )
    return outs[0], outs[1], outs[2], outs[3:]


def bundles(idx, columns, hidden, half, n_dp):
    rows, hid = hidden.shape
    dpc = half // n_dp

    def body(idx_ref, columns_ref, hidden_ref, *refs):
        out, cond_s = refs[:n_dp], refs[n_dp]

        @pl.when(idx_ref[1] == 0)
        def _():
            fill_bundle(out, 0, columns_ref, hidden_ref, cond_s, idx_ref[2])

    return whole(
        body,
        "bundles",
        [(idx, pltpu.SMEM)] + on_vmem([columns, hidden]),
        [((rows, hid + dpc), BF)] * n_dp,
        [pltpu.VMEM((n_dp, rows, dpc), BF)],
    )


def fill_bundle(out, at, columns_ref, hidden_ref, cond_s, d):
    n_dp, _, dpc = cond_s.shape
    hid = hidden_ref.shape[1]
    for j in range(n_dp):
        cond_s[j] = columns_ref[:, j * dpc : (j + 1) * dpc]
    for k in range(n_dp):
        out[k][:, at : at + hid] = hidden_ref[...]
        out[k][:, at + hid : at + hid + dpc] = cond_s[d ^ k]


def couple(chunks, columns, half, cot, deps):
    n = len(chunks)
    n_cot = len(cot)
    rows, two_hb = chunks[0].shape
    hb = two_hb // 2

    def body(*refs):
        parts = refs[:n]
        cots = refs[n : n + n_cot]
        columns_ref, st_ref, log_ref = refs[n + n_cot :]
        raw = parts[0][:, :hb].astype(F32)
        shift = parts[0][:, hb:].astype(F32)
        for k in range(1, n):
            raw = raw + parts[k][:, :hb].astype(F32)
            shift = shift + parts[k][:, hb:].astype(F32)
        arg = raw + 2.0
        scale = sigmoid(arg)
        keep = 1.0 - scale
        cot = cots[0][...].astype(F32)
        for c in cots[1:]:
            cot = cot + c[...].astype(F32)
        cot = cot.astype(BF).astype(F32)
        grad_raw = cot * (columns_ref[:, half:].astype(F32) + shift) * scale * keep - keep
        st_ref[:, :hb] = grad_raw.astype(BF)
        st_ref[:, hb:] = (cot * scale).astype(BF)
        logs = jnp.minimum(arg, 0.0) - jnp.log(1.0 + jnp.exp(-jnp.abs(arg)))
        log_ref[...] = jnp.sum(logs, axis=0, keepdims=True)

    return whole(
        body,
        "couple",
        on_vmem(list(chunks) + list(cot) + [columns]),
        [((rows, two_hb), BF), ((1, hb), F32)],
        deps=deps,
    )


def fill_pack(pack, st_s, d, n_dp, m, hid, hb):
    for j in range(n_dp):
        for i in range(m):
            pack[j][:, hid + i * hb : hid + (i + 1) * hb] = st_s[(d ^ j) * m + i]


def order_st(st_ref, st_s, t, n, hb):
    for k in range(n):
        st_s[t ^ k] = st_ref[k][:, :hb]
        st_s[n + (t ^ k)] = st_ref[k][:, hb:]


def hidden_cotangent(st_s, slope_ref, proj_in, proj_ref, out_ref, n, hb, hid):
    for cols in tiles_of(hid):
        acc = None
        for k in range(2 * n):
            if cols.start == 0:
                proj_in[k].wait()
            part = dot_nn(st_s[k], proj_ref[k * hb : (k + 1) * hb, cols])
            acc = part if acc is None else acc + part
        out_ref[:, cols] = (acc * slope_ref[:, cols]).astype(BF)


def mixed_part(pre, extra, shift_cot, lift_ref, part_s, n, hb):
    for b in range(n):
        part = dot_nt(pre, lift_ref[b * hb : (b + 1) * hb, :])
        part_s[:, b * hb : (b + 1) * hb] = (part + extra(b)).astype(BF)
    part_s[:, n * hb :] = shift_cot


def natural_columns(part_ref, inv_ref, hot_s, first, count, hb, store):
    width = part_ref.shape[1]
    span = span_of(width)

    def one(q, _):
        row = inv_ref[:, pl.ds(pl.multiple_of(q * hb, hb), hb)]
        for i in range(0, width, span):
            fill_hot(hot_s, i, row, float(i), span)
        store(q, dot_nn(part_ref[...], hot_s[...]).astype(BF))
        return 0

    lax.fori_loop(first, first + count, one, 0)


def backward_one(idx, st, ca, slope, inv, lift, proj, width, n):
    rows, two_hb = st[0].shape
    hb = two_hb // 2
    hid = lift.shape[1]

    def body(idx_ref, *refs):
        st_ref = refs[:n]
        ca_ref, slope_ref, inv_ref, lift_h, proj_h = refs[n : n + 5]
        pre_ref, part_ref, nat_ref = refs[n + 5 : n + 8]
        second_out = refs[n + 8 : 2 * n + 8]
        st_s, hot_s, lift_ref, proj_ref, lift_sem, proj_sem = refs[-6:]
        t = idx_ref[0]
        proj_in = loads(proj_h, proj_ref, proj_sem, 2 * n)
        lift_in = loads(lift_h, lift_ref, lift_sem, n)
        for copy in proj_in + lift_in:
            copy.start()
        order_st(st_ref, st_s, t, n, hb)
        hidden_cotangent(st_s, slope_ref, proj_in, proj_ref, pre_ref, n, hb, hid)
        for copy in lift_in:
            copy.wait()
        mixed_part(
            pre_ref[...], lambda b: jnp.where(t == b, ca_ref[...].astype(F32), 0.0),
            st_ref[0][:, hb:], lift_ref, part_ref, n, hb,
        )

        def store(q, block):
            nat_ref[q - n] = block

        natural_columns(part_ref, inv_ref, hot_s, n, n, hb, store)
        for k in range(n):
            second_out[k][...] = nat_ref[t ^ k]

    outs = whole(
        body,
        "backward_one",
        [(idx, pltpu.SMEM)]
        + on_vmem(list(st) + [ca, slope, inv])
        + [(lift, pltpu.HBM), (proj, pltpu.HBM)],
        [((rows, hid), BF), ((rows, width), BF), ((n, rows, hb), BF)] + [((rows, hb), BF)] * n,
        [
            pltpu.VMEM((2 * n, rows, hb), BF),
            pltpu.VMEM((width, hb), BF),
            pltpu.VMEM(lift.shape, BF),
            pltpu.VMEM(proj.shape, BF),
            pltpu.SemaphoreType.DMA((n,)),
            pltpu.SemaphoreType.DMA((2 * n,)),
        ],
    )
    return outs[0], outs[1], outs[2], outs[3:]


def packs_one(idx, st, pre, columns, hidden, half, n_dp, deps):
    n = len(st)
    rows, two_hb = st[0].shape
    hb = two_hb // 2
    hid = pre.shape[1]
    m = 2 * n // n_dp
    dpc = half // n_dp

    def body(idx_ref, *refs):
        st_ref = refs[:n]
        pre_ref, columns_ref, hidden_ref = refs[n : n + 3]
        pack = refs[n + 3 : n + 3 + n_dp]
        st_s, cond_s = refs[-2:]

        @pl.when(idx_ref[1] != 0)
        def _():
            order_st(st_ref, st_s, idx_ref[0], n, hb)
            for j in range(n_dp):
                pack[j][:, :hid] = pre_ref[...]
            fill_pack(pack, st_s, idx_ref[2], n_dp, m, hid, hb)
            fill_bundle(pack, hid + m * hb, columns_ref, hidden_ref, cond_s, idx_ref[2])

    return whole(
        body,
        "packs_one",
        [(idx, pltpu.SMEM)] + on_vmem(list(st) + [pre, columns, hidden]),
        [((rows, 2 * hid + m * hb + dpc), BF)] * n_dp,
        [pltpu.VMEM((2 * n, rows, hb), BF), pltpu.VMEM((n_dp, rows, dpc), BF)],
        deps=deps,
    )


def backward_one_rest(idx, part, inv, n, deps):
    rows, width = part.shape
    hb = inv.shape[1] // (2 * n)

    def body(idx_ref, part_ref, inv_ref, nat_ref, hot_s):
        @pl.when(idx_ref[1] != 0)
        def _():
            def store(q, block):
                nat_ref[q] = block

            natural_columns(part_ref, inv_ref, hot_s, 0, n, hb, store)

    return whole(
        body,
        "backward_one_rest",
        [(idx, pltpu.SMEM)] + on_vmem([part, inv]),
        [((n, rows, hb), BF)],
        [pltpu.VMEM((width, hb), BF)],
        deps=deps,
    )[0]


def chunks_of(idx, stack, deps):
    n, rows, cols = stack.shape[0] // 2, stack.shape[1], stack.shape[2]

    def body(idx_ref, stack_ref, *out):
        for k in range(n):
            for i in range(2):
                out[k][:, i * cols : (i + 1) * cols] = stack_ref[2 * (idx_ref[0] ^ k) + i]

    return whole(
        body,
        "chunks_of",
        [(idx, pltpu.SMEM)] + on_vmem([stack]),
        [((rows, 2 * cols), BF)] * n,
        deps=deps,
    )


def backward_zero(idx, st, slope, proj, n, n_dp, deps):
    rows, two_hb = st[0].shape
    hb = two_hb // 2
    hid = proj.shape[1]
    m = 2 * n // n_dp

    def body(idx_ref, *refs):
        st_ref = refs[:n]
        slope_ref, proj_h = refs[n : n + 2]
        pack = refs[n + 2 : n + 2 + n_dp]
        st_s, proj_ref, proj_sem = refs[-3:]

        @pl.when(idx_ref[1] == 0)
        def _():
            proj_in = loads(proj_h, proj_ref, proj_sem, 2 * n)
            for copy in proj_in:
                copy.start()
            order_st(st_ref, st_s, idx_ref[0], n, hb)
            hidden_cotangent(st_s, slope_ref, proj_in, proj_ref, pack[0], n, hb, hid)
            for j in range(1, n_dp):
                pack[j][:, :hid] = pack[0][:, :hid]
            fill_pack(pack, st_s, idx_ref[2], n_dp, m, hid, hb)

    return whole(
        body,
        "backward_zero",
        [(idx, pltpu.SMEM)] + on_vmem(list(st) + [slope]) + [(proj, pltpu.HBM)],
        [((rows, hid + m * hb), BF)] * n_dp,
        [
            pltpu.VMEM((2 * n, rows, hb), BF),
            pltpu.VMEM(proj.shape, BF),
            pltpu.SemaphoreType.DMA((2 * n,)),
        ],
        deps=deps,
    )


def natural_shares(idx, st_own, pack, low_one, inv, lift, low, high, width, n):
    rows, two_hb = st_own.shape
    hb = two_hb // 2
    hid = lift.shape[1]

    def body(idx_ref, st_ref, pack_ref, *refs):
        got_ref, inv_ref, lift_h, low_ref, high_ref, nat_s, part_s, hot_s, lift_ref, lift_sem = refs

        @pl.when(idx_ref[1] == 0)
        def _():
            lift_in = loads(lift_h, lift_ref, lift_sem, n)
            for copy in lift_in:
                copy.start()
            for copy in lift_in:
                copy.wait()
            mixed_part(
                pack_ref[:, :hid], lambda b: got_ref[b].astype(F32), st_ref[:, hb:], lift_ref,
                part_s, n, hb,
            )

            def store(q, block):
                nat_s[q] = block

            natural_columns(part_s, inv_ref, hot_s, 0, 2 * n, hb, store)

        @pl.when(idx_ref[1] != 0)
        def _():
            for q in range(n):
                nat_s[q] = low_ref[q]
                nat_s[n + q] = high_ref[q]

    return whole(
        body,
        "natural_shares",
        [(idx, pltpu.SMEM)]
        + on_vmem([st_own, pack, low_one, inv])
        + [(lift, pltpu.HBM)]
        + on_vmem([low, high]),
        [((2 * n, rows, hb), BF)],
        [
            pltpu.VMEM((rows, width), BF),
            pltpu.VMEM((width, hb), BF),
            pltpu.VMEM(lift.shape, BF),
            pltpu.SemaphoreType.DMA((n,)),
        ],
    )[0]


def fetch(idx_ref, kind, bund, zero, one, lhs, rhs, sem, wait):
    n_dp = len(one)
    rows = one[0].shape[0]
    hid = rhs.shape[1]
    width = lhs.shape[1]
    st_cols = zero[0].shape[1] - hid

    def act(src, first, dst, k, of):
        copy = pltpu.make_async_copy(
            src.at[:, pl.ds(first, dst.shape[1])],
            dst.at[pl.ds(k * rows, rows)],
            sem.at[of * n_dp + k],
        )
        if wait:
            copy.wait()
        else:
            copy.start()

    def act_all(pack, late, late_at):
        for k in range(n_dp):
            if kind == "proj":
                act(pack[k], hid, lhs, k, 0)
                act(late[k], late_at, rhs, k, 1)
            else:
                act(late[k], late_at + hid, lhs, k, 0)
                act(pack[k], 0, rhs, k, 1)

    @pl.when(idx_ref[1] == 0)
    def _():
        act_all(zero, bund, 0)

    @pl.when(idx_ref[1] != 0)
    def _():
        act_all(one, one, hid + st_cols)


def factors(kind, bund, zero, hid):
    n_dp = len(zero)
    tokens = n_dp * zero[0].shape[0]
    width = (zero if kind == "proj" else bund)[0].shape[1] - hid
    return [
        pltpu.VMEM((tokens, width), BF),
        pltpu.VMEM((tokens, hid), BF),
        pltpu.SemaphoreType.DMA((2 * n_dp,)),
    ]


def weight_squares(idx, lift_mask, proj_mask, bund, zero, one, logs, hid):
    n_dp = len(zero)
    lift_s = factors("lift", bund, zero, hid)
    proj_s = factors("proj", bund, zero, hid)

    def body(idx_ref, lift_mask_ref, proj_mask_ref, log_ref, *refs):
        packs = [refs[i * n_dp : (i + 1) * n_dp] for i in range(3)]
        refs = refs[3 * n_dp :]
        sum_ref, sq_s = refs[:2]
        groups = (("proj", proj_mask_ref, refs[2:5]), ("lift", lift_mask_ref, refs[5:8]))
        for wait in (False, True):
            for kind, _, (lhs, rhs, sem) in groups:
                fetch(idx_ref, kind, *packs, lhs, rhs, sem, wait)
        sq_s[...] = jnp.zeros_like(sq_s)
        d = idx_ref[2]
        for kind, mask, (lhs, rhs, _) in groups:
            n_rows = lhs.shape[1]
            first = d * (n_rows // BLK)
            tile = min(512, n_rows)
            for cols in tiles_of(hid):
                for r in range(0, n_rows, tile):
                    grad = dot_tn(lhs[:, r : r + tile], rhs[:, cols])
                    total = None
                    for i in range(grad.shape[0] // BLK):
                        for j in range(grad.shape[1] // BLK):
                            part = grad[i * BLK : (i + 1) * BLK, j * BLK : (j + 1) * BLK]
                            kept = mask[first + r // BLK + i, cols.start // BLK + j] > 0
                            part = jnp.sum((part * part).reshape(BLK // 8, 8, BLK), axis=0)
                            part = jnp.where(kept, part, 0.0)
                            total = part if total is None else total + part
                    sq_s[...] += total
        lane = lax.broadcasted_iota(jnp.int32, sum_ref.shape, 1)
        square = jnp.sum(sq_s[...])
        log_sum = jnp.sum(log_ref[...])
        sum_ref[...] = jnp.where(lane == 0, square, jnp.where(lane == 1, log_sum, 0.0))

    n_all = lax.axis_size("dp") * lax.axis_size("tensor") * lax.axis_size("layers")
    return whole(
        body,
        "weight_squares",
        [(idx, pltpu.SMEM), (lift_mask, pltpu.SMEM), (proj_mask, pltpu.SMEM), (logs, pltpu.VMEM)]
        + [(x, pltpu.HBM) for x in list(bund) + list(zero) + list(one)],
        [((n_all, BLK), F32)],
        [pltpu.VMEM((8, BLK), F32)] + proj_s + lift_s,
    )[0]


def adam(idx, sums, kind, mask, bund, zero, one, moment, square, hid, dep):
    n_dp = len(zero)
    n_rows, n_cols = moment.shape
    tile = min(256, n_rows)
    inv_one = 1.0 / (1.0 - beta_one**ADAM_STEP)
    inv_two = 1.0 / (1.0 - beta_two**ADAM_STEP)

    def body(idx_ref, mask_ref, sums_ref, dep_ref, *refs):
        packs = [refs[i * n_dp : (i + 1) * n_dp] for i in range(3)]
        m_ref, v_ref, first_ref, second_ref, upd_ref, lhs, rhs, sem = refs[3 * n_dp :]
        step = pl.program_id(0)

        @pl.when(step == 0)
        def _():
            for wait in (False, True):
                fetch(idx_ref, kind, *packs, lhs, rhs, sem, wait)

        row = idx_ref[2] * (n_rows // BLK) + step * (tile // BLK)
        square_total = jnp.sum(sums_ref[:, 0:1], axis=0, keepdims=True)
        factor = jnp.minimum(1.0, CLIP / (jnp.sqrt(square_total) + 1e-06))
        left = lhs[:, pl.ds(pl.multiple_of(step * tile, tile), tile)]
        for cols in tiles_of(n_cols):
            grad = dot_tn(left, rhs[:, cols])
            for i in range(tile // BLK):
                for j in range(grad.shape[1] // BLK):
                    at = (
                        slice(i * BLK, (i + 1) * BLK),
                        slice(cols.start + j * BLK, cols.start + (j + 1) * BLK),
                    )
                    kept = mask_ref[row + i, cols.start // BLK + j] > 0
                    g = grad[i * BLK : (i + 1) * BLK, j * BLK : (j + 1) * BLK] * factor
                    old_m, old_v = m_ref[at], v_ref[at]
                    new_m = jnp.where(kept, beta_one * old_m + (1.0 - beta_one) * g, old_m)
                    new_v = jnp.where(kept, beta_two * old_v + (1.0 - beta_two) * g * g, old_v)
                    spread = new_v * inv_two
                    upd = (new_m * inv_one) / (spread * lax.rsqrt(spread) + adam_eps)
                    first_ref[at] = new_m
                    second_ref[at] = new_v
                    upd_ref[at] = jnp.where(kept, upd, 0.0)

    spec = pl.BlockSpec((tile, n_cols), lambda i: (i, 0))
    return pl.pallas_call(
        body,
        grid=(n_rows // tile,),
        in_specs=[sspec()] * 2
        + [vspec()]
        + [pl.BlockSpec(memory_space=pl.ANY)]
        + [pl.BlockSpec(memory_space=pltpu.HBM)] * (3 * n_dp)
        + [spec] * 2,
        out_specs=[spec] * 3,
        out_shape=[pltpu.HBM(moment.shape, F32)] * 3,
        scratch_shapes=factors(kind, bund, zero, hid),
        compiler_params=pltpu.CompilerParams(vmem_limit_bytes=VMEM_LIMIT),
        name="adam_" + kind,
    )(
        idx, mask, sums, dep, *map(in_hbm, (*bund, *zero, *one)), in_hbm(moment), in_hbm(square)
    )


def total(parts):
    acc = parts[0].astype(F32)
    for p in parts[1:]:
        acc = acc + p.astype(F32)
    return acc


def per_device(
    section_input,
    out_cotangent,
    lift_weight,
    proj_weight,
    lift_mask,
    proj_mask,
    channel_perm,
    lift_moment,
    lift_square,
    proj_moment,
    proj_square,
):
    n = lax.axis_size("tensor")
    n_dp = lax.axis_size("dp")
    t = lax.axis_index("tensor")
    section = lax.axis_index("layers")
    d = lax.axis_index("dp")
    idx = jnp.stack([t, section, d]).astype(jnp.int32)
    perm = channel_perm[0]
    feat = perm.shape[0]
    half = feat // 2
    hb = half // n
    rows = section_input.shape[1]
    lift_mask, proj_mask = lift_mask[0], proj_mask[0]

    with jax.named_scope("tokens_exchange"):
        tokens = gather_tensor(section_input[0], None)
    with jax.named_scope("cotangent_exchange"):
        ca, cb = spread_halves(out_cotangent[:, :hb], out_cotangent[:, hb:], t)

    own = lax.dynamic_slice_in_dim(perm, half + t * hb, hb, 0)
    perm_cols = jnp.concatenate([perm[:half], own])[None].astype(F32)
    width = perm_cols.shape[1]
    lift, proj = prep_weights(lift_mask, proj_mask, lift_weight[0], proj_weight[0])
    hid = lift.shape[1]

    slope, columns, hidden, shared = forward(
        idx, tokens, perm_cols, lift, proj, n, (ca, cb)
    )
    with jax.named_scope("shared_exchange"):
        shared = scatter_tensor(shared, None)
    with jax.named_scope("hidden_exchange"):
        bund = scatter_dp(bundles(idx, columns, hidden, half, n_dp), 0)
    inv = prep_inverse(perm_cols, feat, (columns,))

    st_own, logs = couple(shared, columns, half, [cb], (inv,) + tuple(bund[1:]))
    with jax.named_scope("st_one_exchange"):
        st = gather_tensor(st_own, 1)
    pre, part, high, second = backward_one(idx, st, ca, slope, inv, lift, proj, width, n)
    with jax.named_scope("down_exchange"):
        cb_zero = down_a_section(second)

    st_own, _ = couple(shared, columns, half, cb_zero, ())
    with jax.named_scope("st_zero_exchange"):
        st_zero = gather_tensor(st_own, 0)
    pack_one = packs_one(idx, st, pre, columns, hidden, half, n_dp, tuple(st_zero))
    with jax.named_scope("dp_one_exchange"):
        pack_one = scatter_dp(pack_one, 1)
    low = backward_one_rest(idx, part, inv, n, tuple(pack_one[1:]))
    with jax.named_scope("down_late_exchange"):
        low_one = lax.ppermute(low, "layers", [(1, 0)])
    pack_zero = backward_zero(idx, st_zero, slope, proj, n, n_dp, ())
    with jax.named_scope("dp_zero_exchange"):
        pack_got = scatter_dp(pack_zero, 0)
    shares = natural_shares(
        idx, st_own, pack_zero[0], low_one, inv, lift, low, high, width, n
    )

    sources = (bund, pack_got, pack_one)
    sums = weight_squares(idx, lift_mask, proj_mask, *sources, logs, hid)
    with jax.named_scope("norm_exchange"):
        sums = lax.all_to_all(
            sums, ("dp", "tensor", "layers"), split_axis=0, concat_axis=0, tiled=True
        )
    shares = chunks_of(idx, shares, (sums,))
    lift_out = adam(
        idx, sums, "lift", lift_mask, *sources, lift_moment[0], lift_square[0], hid, shares[0]
    )
    with jax.named_scope("input_exchange"):
        shares = scatter_tensor(shares, None)
    proj_out = adam(
        idx, sums, "proj", proj_mask, *sources, proj_moment[0], proj_square[0], hid, shares[0]
    )

    input_grad = total(shares)[None]
    by_section = sums.reshape(n_dp * n, -1, BLK)
    log_total = jnp.sum(lax.dynamic_index_in_dim(by_section, section, 1, False)[:, 1])
    log_det = (log_total / (rows * n_dp * half)).reshape(1)
    return (
        input_grad,
        log_det,
        lift_out[0][None],
        lift_out[1][None],
        lift_out[2][None],
        proj_out[0][None],
        proj_out[1][None],
        proj_out[2][None],
    )


def solution(mesh):
    return jax.shard_map(
        per_device,
        mesh=mesh,
        in_specs=(
            P("layers", "dp", "tensor"),
            P("dp", "tensor"),
            P("layers", None, "tensor"),
            P("layers", None, "tensor"),
            P("layers", None, "tensor"),
            P("layers", None, "tensor"),
            P("layers", None),
            P("layers", "dp", "tensor"),
            P("layers", "dp", "tensor"),
            P("layers", "dp", "tensor"),
            P("layers", "dp", "tensor"),
        ),
        out_specs=(
            P("layers", "dp", "tensor"),
            P("layers"),
            P("layers", "dp", "tensor"),
            P("layers", "dp", "tensor"),
            P("layers", "dp", "tensor"),
            P("layers", "dp", "tensor"),
            P("layers", "dp", "tensor"),
            P("layers", "dp", "tensor"),
        ),
        check_vma=False,
    )
```

time: 400 us -> 199 us (0.50)
  waiting for transfers between devices: 132 us -> 46.7 us
  blocking collectives: 80.9 us -> 0 us
  Pallas kernels: 0 us -> 79.4 us
  local copies, waits for them, and re-layouts: 74.8 us -> 8.23 us
  starting transfers between devices: 9.94 us -> 57.8 us
  matrix products: 43.8 us -> 0 us
  other arithmetic: 38.6 us -> 2.72 us
  between operations: 19 us -> 3.11 us
    psum x2 -> x0, blocking collectives: 80.9 us -> none  [the longest x1 41.7 us: per_device(): log_total = lax.psum(log_part, ('dp', 'tensor'))]
    pallas_call x0 -> x15, Pallas kernels: none -> 79.4 us  [the longest x12 48.7 us: whole(): pl.pallas_call(run, in_specs=specs + [pl.BlockSpec(memory_space=pl.ANY)]...]
    psum x3 -> x0, waiting for transfers between devices: 72.9 us -> none  [the longest x1 50.7 us: per_device(): lax.psum(contract_cols(hidden, proj_eff).astype(jnp.bfloat16), 'tensor')]
    ppermute x1 -> x31, starting transfers between devices: 1.5 us -> 55.2 us  [the longest x17 28.2 us: over_tensor(): return lax.ppermute(x, ('tensor', 'layers'), route)]
    dot_general x7 -> x0, matrix products: 43.8 us -> none  [the longest x3 24.8 us: contract_cols(): lax.dot_general(left_mat, right_mat, (((1,), (1,)), ((), ())), preferred_...]
    ppermute x1 -> x31, waiting for transfers between devices: 3.35 us -> 46.7 us  [the longest x17 18.8 us: over_tensor(): return lax.ppermute(x, ('tensor', 'layers'), route)]
    all_gather x4 -> x0, waiting for transfers between devices: 43.1 us -> none  [the longest x1 27.9 us: per_device(): lax.all_gather(section_input[0], 'tensor', axis=1, tiled=True)]
    gather x5 -> x0, local copies, waits for them, and re-layouts: 33.1 us -> none  [the longest x2 17.4 us: per_device(): early_grad = jnp.take(early_mixed, inverse, axis=1)]
  transfers between devices with their start and end apart: 10 -> 32, of which waited for: 7 -> 9; matrix products, arithmetic and copies ran while one was open for 18% -> 2% of each run, Pallas kernels for 0% -> 30%
where the time goes in v1:
time: 199 us; the launch traced here: 198 us
  Pallas kernels  79.4 us (40%)
  starting transfers between devices  57.8 us (29%)
  waiting for transfers between devices  46.7 us (23%)
  local copies, waits for them, and re-layouts  8.23 us (4%)
  between operations  3.11 us (2%)
  other arithmetic  2.72 us (1%)
    pallas_call x12, Pallas kernels, whole(): pl.pallas_call(run, in_specs=specs + [pl.BlockSpec(memory_space=pl.ANY)]...  48.7 us
    ppermute x17, starting transfers between devices, over_tensor(): return lax.ppermute(x, ('tensor', 'layers'), route)  28.2 us
    ppermute x9, starting transfers between devices, over_dp(): return lax.ppermute(x, ('dp', 'layers'), route)  20.6 us
    ppermute x17, waiting for transfers between devices, over_tensor(): return lax.ppermute(x, ('tensor', 'layers'), route)  18.8 us
    pallas_call x2, Pallas kernels, adam(): pl.pallas_call(body, grid=(n_rows // tile,), in_specs=[sspec()] * 2 + [vs...  18.1 us
    pallas_call x1, Pallas kernels, prep_weights(): pl.pallas_call(body, grid=(steps,), in_specs=[sspec(), sspec()] + specs,...  12.6 us
    ppermute x3, waiting for transfers between devices, down_a_section(): lax.ppermute(chunks[k], ('tensor', 'layers'), [(i * m + 1, j * m) for i,...  9.71 us
    ppermute x1, waiting for transfers between devices, down_a_section(): got[0] = lax.ppermute(chunks[0], 'layers', [(1, 0)])  9.3 us
  transfers between devices with their start and end apart: 32, of which 9 were waited for; matrix products, arithmetic and copies ran while one was open for 2% of the time, Pallas kernels for 30%

profile of v1, /device:TPU:0, one launch (start us, length us, event | category | flops | bytes accessed | tf_op | source)
XLA Modules:
  0.0 197.9 jit_solution(6454560168823257563)
XLA Ops:
  0.6 5.1 %collective-permute-start.2 = (bf16[128,1024]{1,0:T(8,128)(2,1)}, bf16[128,1024]{1,0:T(8,128)(2,1)S(1)}, u32[]{:S(2)}, u32[]{:S(2)}) collective-permute-start(bf16[128,1024]{1,0:T(8,128)(2,1)} %bitcast.34), channel_id=1, source_target_pairs={{0,6},{1,7},{2,4},{3,5},{4,2},{5,3},{6,0},{7,1},{8,14},{9,15},{10,... | collective-permute-start | bytes 786440 | tf_op jit(solution)/shard_map/tokens_exchange/ppermute | solution.py:57
  11.8 12.6 %prep_weights.1 = (bf16[2048,1024]{1,0:T(8,128)(2,1)}, bf16[4096,1024]{1,0:T(8,128)(2,1)}) custom-call(s32[16,8]{1,0:T(8,128)S(1)} %copy.24.lift_mask_ref.refs_1_.mask_ref, s32[32,8]{1,0:T(8,128)S(1)} %bitcast.31, bf16[2048,1024]{1,0:T(8,128)(2,1)} %bitcast.41, bf16[4096,1024]{1,0:T(8,128)(2,1)} %bitcast.38), custom_call_target="tpu_custom_call" | custom-call | tf_op jit(solution)/shard_map/prep_weights/pallas_call | solution.py:200
  24.4 4.8 %collective-permute-done.1.refs_3_ = bf16[128,1024]{1,0:T(8,128)(2,1)S(1)} collective-permute-done((bf16[128,1024]{1,0:T(8,128)(2,1)}, bf16[128,1024]{1,0:T(8,128)(2,1)S(1)}, u32[]{:S(2)}, u32[]{:S(2)}) %collective-permute-start.1) | collective-permute-done | bytes 262176 | tf_op jit(solution)/shard_map/tokens_exchange/ppermute | solution.py:57
  29.2 8.7 %forward.1 = (f32[128,1024]{1,0:T(8,128)S(1)}, bf16[128,2560]{1,0:T(8,128)(2,1)S(1)}, bf16[128,1024]{1,0:T(8,128)(2,1)S(1)}, bf16[128,1024]{1,0:T(8,128)(2,1)S(1...) custom-call(s32[3]{0:T(128)S(1)} %pad_add_fusion.refs_0_.idx_ref, ...), custom_call_target="tpu_custom_call" | custom-call | tf_op jit(solution)/shard_map/forward/pallas_call | solution.py:125
  38.7 3.4 %collective-permute-start.8 = (bf16[128,1536]{1,0:T(8,128)(2,1)S(1)}, bf16[128,1536]{1,0:T(8,128)(2,1)S(1)}, u32[]{:S(2)}, u32[]{:S(2)}) collective-permute-start(bf16[128,1536]{1,0:T(8,128)(2,1)S(1)} %get-tuple-element.57), channel_id=1, source_target_pairs={{0,8},{8,0},{16,24},{24,16},{2,10},{10,2},{18,26},{26,18},{4,12},{... | collective-permute-start | bytes 1179656 | tf_op jit(solution)/shard_map/hidden_exchange/ppermute | solution.py:64
  42.1 3.4 %collective-permute-start.9 = (bf16[128,1536]{1,0:T(8,128)(2,1)S(1)}, bf16[128,1536]{1,0:T(8,128)(2,1)S(1)}, u32[]{:S(2)}, u32[]{:S(2)}) collective-permute-start(bf16[128,1536]{1,0:T(8,128)(2,1)S(1)} %get-tuple-element.58), channel_id=1, source_target_pairs={{0,16},{8,24},{16,0},{24,8},{2,18},{10,26},{18,2},{26,10},{4,20},{... | collective-permute-start | bytes 1179656 | tf_op jit(solution)/shard_map/hidden_exchange/ppermute | solution.py:64
  47.9 3.3 %collective-permute-start.6 = (bf16[128,1024]{1,0:T(8,128)(2,1)S(1)}, bf16[128,1024]{1,0:T(8,128)(2,1)S(1)}, u32[]{:S(2)}, u32[]{:S(2)}) collective-permute-start(bf16[128,1024]{1,0:T(8,128)(2,1)S(1)} %get-tuple-element.53), channel_id=1, source_target_pairs={{0,4},{1,5},{2,6},{3,7},{4,0},{5,1},{6,2},{7,3},{8,12},{9,13},{10,... | collective-permute-start | bytes 786440 | tf_op jit(solution)/shard_map/shared_exchange/ppermute | solution.py:57
  52.4 7.4 %prep_inverse.1.refs_6_.refs_7_.refs_2_.refs_4_ = f32[1,4096]{1,0:T(1,128)S(1)} custom-call(f32[1,2560]{1,0:T(1,128)S(1)} %add_convert_fusion.refs_5_.refs_0_, bf16[128,2560]{1,0:T(8,128)(2,1)S(1)} %get-tuple-element.55.refs_1_.refs_5_.refs_8_.refs_6_), custom_call_target="tpu_custom_call" | custom-call | tf_op jit(solution)/shard_map/prep_inverse/pallas_call | solution.py:125
  59.8 6.1 %collective-permute-done.6.refs_2_ = bf16[128,1024]{1,0:T(8,128)(2,1)S(1)} collective-permute-done((bf16[128,1024]{1,0:T(8,128)(2,1)S(1)}, bf16[128,1024]{1,0:T(8,128)(2,1)S(1)}, u32[]{:S(2)}, u32[]{:S(2)}) %collective-permute-start.6) | collective-permute-done | bytes 262176 | tf_op jit(solution)/shard_map/shared_exchange/ppermute | solution.py:57
  68.4 9.4 %backward_one.1 = (bf16[128,1024]{1,0:T(8,128)(2,1)S(1)}, bf16[128,2560]{1,0:T(8,128)(2,1)S(1)}, bf16[4,128,512]{2,1,0:T(8,128)(2,1)S(1)}, bf16[128,512]{1,0:T(8...) custom-call(s32[3]{0:T(128)S(1)} %pad_add_fusion.refs_0_.idx_ref, ...), custom_call_target="tpu_custom_call" | custom-call | tf_op jit(solution)/shard_map/backward_one/pallas_call | solution.py:125
  83.1 9.3 %collective-permute-done.14.refs_4_ = bf16[128,512]{1,0:T(8,128)(2,1)S(1)} collective-permute-done((bf16[128,512]{1,0:T(8,128)(2,1)S(1)}, bf16[128,512]{1,0:T(8,128)(2,1)S(1)}, u32[]{:S(2)}, u32[]{:S(2)}) %collective-permute-start.14) | collective-permute-done | bytes 131104 | tf_op jit(solution)/shard_map/down_exchange/ppermute | solution.py:96
  95.1 3.8 %collective-permute-done.16.refs_6_ = bf16[128,512]{1,0:T(8,128)(2,1)S(1)} collective-permute-done((bf16[128,512]{1,0:T(8,128)(2,1)S(1)}, bf16[128,512]{1,0:T(8,128)(2,1)S(1)}, u32[]{:S(2)}, u32[]{:S(2)}) %collective-permute-start.16) | collective-permute-done | bytes 131104 | tf_op jit(solution)/shard_map/down_exchange/ppermute | solution.py:91
  98.9 3.2 %collective-permute-done.17.refs_7_ = bf16[128,512]{1,0:T(8,128)(2,1)S(1)} collective-permute-done((bf16[128,512]{1,0:T(8,128)(2,1)S(1)}, bf16[128,512]{1,0:T(8,128)(2,1)S(1)}, u32[]{:S(2)}, u32[]{:S(2)}) %collective-permute-start.17) | collective-permute-done | bytes 131104 | tf_op jit(solution)/shard_map/down_exchange/ppermute | solution.py:91
  104.8 4.9 %collective-permute-start.19 = (bf16[128,1024]{1,0:T(8,128)(2,1)S(1)}, bf16[128,1024]{1,0:T(8,128)(2,1)S(1)}, u32[]{:S(2)}, u32[]{:S(2)}) collective-permute-start(bf16[128,1024]{1,0:T(8,128)(2,1)S(1)} %get-tuple-element.66.refs_1_.refs_8_), channel_id=1, source_target_pairs={{0,4},{2,6},{4,0},{6,2},{8,12},{10,14},{12,8},{14,10},{16,20},{18,... | collective-permute-start | bytes 786440 | tf_op jit(solution)/shard_map/st_zero_exchange/ppermute | solution.py:57
  109.7 3.3 %collective-permute-start.18 = (bf16[128,1024]{1,0:T(8,128)(2,1)S(1)}, bf16[128,1024]{1,0:T(8,128)(2,1)S(1)}, u32[]{:S(2)}, u32[]{:S(2)}) collective-permute-start(bf16[128,1024]{1,0:T(8,128)(2,1)S(1)} %get-tuple-element.66.refs_1_.refs_8_), channel_id=1, source_target_pairs={{0,2},{2,0},{4,6},{6,4},{8,10},{10,8},{12,14},{14,12},{16,18},{18,... | collective-permute-start | bytes 786440 | tf_op jit(solution)/shard_map/st_zero_exchange/ppermute | solution.py:57
  113.1 7.6 %collective-permute-done.19.refs_3_.refs_10_ = bf16[128,1024]{1,0:T(8,128)(2,1)S(1)} collective-permute-done((bf16[128,1024]{1,0:T(8,128)(2,1)S(1)}, bf16[128,1024]{1,0:T(8,128)(2,1)S(1)}, u32[]{:S(2)}, u32[]{:S(2)}) %collective-permute-start.19) | collective-permute-done | bytes 262176 | tf_op jit(solution)/shard_map/st_zero_exchange/ppermute | solution.py:57
  125.2 5.1 %backward_zero.1 = (bf16[128,2048]{1,0:T(8,128)(2,1)S(1)}, bf16[128,2048]{1,0:T(8,128)(2,1)S(1)}, bf16[128,2048]{1,0:T(8,128)(2,1)S(1)}, bf16[128,2048]{1,0:T(8,128)(2,1)S(1)}) custom-call(s32[3]{0:T(128)S(1)} %copy-done.20, bf16[128,1024]{1,0:T(8,128)(2,1)S(1)} %get-tuple-element.66.refs_1_.refs_8_, ...), custom_call_target="tpu_custom_call" | custom-call | tf_op jit(solution)/shard_map/backward_zero/pallas_call | solution.py:125
  130.3 3.4 %collective-permute-start.25 = (bf16[128,2048]{1,0:T(8,128)(2,1)S(1)}, bf16[128,2048]{1,0:T(8,128)(2,1)S(1)}, u32[]{:S(2)}, u32[]{:S(2)}) collective-permute-start(bf16[128,2048]{1,0:T(8,128)(2,1)S(1)} %get-tuple-element.76), channel_id=1, source_target_pairs={{0,8},{8,0},{16,24},{24,16},{2,10},{10,2},{18,26},{26,18},{4,12},{... | collective-permute-start | bytes 1572872 | tf_op jit(solution)/shard_map/dp_zero_exchange/ppermute | solution.py:64
  133.7 3.4 %collective-permute-start.26 = (bf16[128,2048]{1,0:T(8,128)(2,1)S(1)}, bf16[128,2048]{1,0:T(8,128)(2,1)S(1)}, u32[]{:S(2)}, u32[]{:S(2)}) collective-permute-start(bf16[128,2048]{1,0:T(8,128)(2,1)S(1)} %get-tuple-element.77), channel_id=1, source_target_pairs={{0,16},{8,24},{16,0},{24,8},{2,18},{10,26},{18,2},{26,10},{4,20},{... | collective-permute-start | bytes 1572872 | tf_op jit(solution)/shard_map/dp_zero_exchange/ppermute | solution.py:64
  141.4 8.9 %collective-permute-done.26.refs_10_.refs_6_ = bf16[128,2048]{1,0:T(8,128)(2,1)S(1)} collective-permute-done((bf16[128,2048]{1,0:T(8,128)(2,1)S(1)}, bf16[128,2048]{1,0:T(8,128)(2,1)S(1)}, u32[]{:S(2)}, u32[]{:S(2)}) %collective-permute-start.26) | collective-permute-done | bytes 524320 | tf_op jit(solution)/shard_map/dp_zero_exchange/ppermute | solution.py:64
  151.3 5.7 %weight_squares.1 = f32[32,128]{1,0:T(8,128)} custom-call(s32[3]{0:T(128)S(1)} %copy-done.20, s32[16,8]{1,0:T(8,128)S(1)} %copy-done.17, s32[32,8]{1,0:T(8,128)S(1)} %bitcast.32, f32[1,512]{1,0:T(1,128)S(1)} %get-tuple-element.74.refs_3_, bf16[128,1536]{1,0:T(8,128)(2,1)} %copy-done.9, bf16[128,1536]{1,0:T(8,128)(2,1)} %copy-done.6, ...), custom_call_target="tpu_custom_call" | custom-call | tf_op jit(solution)/shard_map/weight_squares/pallas_call | solution.py:125
  162.3 8.9 %natural_shares.1.refs_1_ = bf16[8,128,512]{2,1,0:T(8,128)(2,1)S(1)} custom-call(s32[3]{0:T(128)S(1)} %copy-done.21, bf16[128,1024]{1,0:T(8,128)(2,1)S(1)} %get-tuple-element.66.refs_1_.refs_8_, bf16[128,2048]{1,0:T(8,128)(2,1)S(1)} %copy-done.4, bf16[4,128,512]{2,1,0:T(8,128)(2,1)} %collective-permute-done.24.refs_3_, ...), custom_call_target="tpu_custom_call" | custom-call | tf_op jit(solution)/shard_map/natural_shares/pallas_call | solution.py:125
  177.7 6.7 %adam_lift.1 = (f32[512,1024]{1,0:T(8,128)}, f32[512,1024]{1,0:T(8,128)}, f32[512,1024]{1,0:T(8,128)}) custom-call(s32[3]{0:T(128)S(1)} %copy-done.22, s32[16,8]{1,0:T(8,128)S(1)} %copy-done.18, f32[32,128]{1,0:T(8,128)S(1)} %bitcast.29, bf16[128,1024]{1,0:T(8,128)(2,1)S(1)} %get-tuple-element.80.dep_ref, bf16[128,1536]{1,0:T(8,128)(2,1)} %copy-done.9, ...), custom_call_target="tpu_custom_call" | custom-call | tf_op jit(solution)/shard_map/adam_lift/pallas_call | solution.py:766
  184.4 11.3 %adam_proj.1 = (f32[1024,1024]{1,0:T(8,128)}, f32[1024,1024]{1,0:T(8,128)}, f32[1024,1024]{1,0:T(8,128)}) custom-call(s32[3]{0:T(128)S(1)} %copy-done.22, s32[32,8]{1,0:T(8,128)S(1)} %bitcast.33, f32[32,128]{1,0:T(8,128)S(1)} %bitcast.30, bf16[128,1024]{1,0:T(8,128)(2,1)S(1)} %get-tuple-element.80.dep_ref, bf16[128,1536]{1,0:T(8,128)(2,1)} %copy-done.9, ...), custom_call_target="tpu_custom_call" | custom-call | tf_op jit(solution)/shard_map/adam_proj/pallas_call | solution.py:766
  (118 shorter events, 45.0 us)
Async XLA Ops:
  0.6 23.8 %collective-permute-start.2 = (bf16[128,1024]{1,0:T(8,128)(2,1)}, bf16[128,1024]{1,0:T(8,128)(2,1)S(1)}, u32[]{:S(2)}, u32[]{:S(2)}) collective-permute-start(bf16[128,1024]{1,0:T(8,128)(2,1)} %bitcast.34), channel_id=1, source_target_pairs={{0,6},{1,7},{2,4},{3,5},{4,2},{5,3},{6,0},{7,1},{8,14},{9,15},{10,... | collective-permute-start | bytes 786440 | tf_op jit(solution)/shard_map/tokens_exchange/ppermute | solution.py:57
  5.7 23.5 %collective-permute-start.1 = (bf16[128,1024]{1,0:T(8,128)(2,1)}, bf16[128,1024]{1,0:T(8,128)(2,1)S(1)}, u32[]{:S(2)}, u32[]{:S(2)}) collective-permute-start(bf16[128,1024]{1,0:T(8,128)(2,1)} %bitcast.35), channel_id=1, source_target_pairs={{0,4},{1,5},{2,6},{3,7},{4,0},{5,1},{6,2},{7,3},{8,12},{9,13},{10,... | collective-permute-start | bytes 786440 | tf_op jit(solution)/shard_map/tokens_exchange/ppermute | solution.py:57
  5.8 23.5 %collective-permute-start = (bf16[128,1024]{1,0:T(8,128)(2,1)}, bf16[128,1024]{1,0:T(8,128)(2,1)S(1)}, u32[]{:S(2)}, u32[]{:S(2)}) collective-permute-start(bf16[128,1024]{1,0:T(8,128)(2,1)} %bitcast.36), channel_id=1, source_target_pairs={{0,2},{1,3},{2,0},{3,1},{4,6},{5,7},{6,4},{7,5},{8,10},{9,11},{10,... | collective-permute-start | bytes 786440 | tf_op jit(solution)/shard_map/tokens_exchange/ppermute | solution.py:57
  7.4 17.0 %collective-permute-start.4 = (bf16[128,512]{1,0:T(8,128)(2,1)S(1)}, bf16[128,512]{1,0:T(8,128)(2,1)S(1)}, u32[]{:S(2)}, u32[]{:S(2)}) collective-permute-start(bf16[128,512]{1,0:T(8,128)(2,1)S(1)} %get-tuple-element.92), channel_id=1, source_target_pairs={{1,3},{3,7},{5,1},{7,5},{9,11},{11,15},{13,9},{15,13},{17,19},{19,... | collective-permute-start | bytes 393224 | tf_op jit(solution)/shard_map/cotangent_exchange/ppermute | solution.py:57
  8.1 16.3 %collective-permute-start.3 = (bf16[128,512]{1,0:T(8,128)(2,1)S(1)}, bf16[128,512]{1,0:T(8,128)(2,1)S(1)}, u32[]{:S(2)}, u32[]{:S(2)}) collective-permute-start(bf16[128,512]{1,0:T(8,128)(2,1)S(1)} %get-tuple-element.93), channel_id=1, source_target_pairs={{1,1},{3,5},{5,3},{7,7},{9,9},{11,13},{13,11},{15,15},{17,17},{19,... | collective-permute-start | bytes 393224 | tf_op jit(solution)/shard_map/cotangent_exchange/ppermute | solution.py:57
  38.7 27.2 %collective-permute-start.8 = (bf16[128,1536]{1,0:T(8,128)(2,1)S(1)}, bf16[128,1536]{1,0:T(8,128)(2,1)S(1)}, u32[]{:S(2)}, u32[]{:S(2)}) collective-permute-start(bf16[128,1536]{1,0:T(8,128)(2,1)S(1)} %get-tuple-element.57), channel_id=1, source_target_pairs={{0,8},{8,0},{16,24},{24,16},{2,10},{10,2},{18,26},{26,18},{4,12},{... | collective-permute-start | bytes 1179656 | tf_op jit(solution)/shard_map/hidden_exchange/ppermute | solution.py:64
  42.1 23.8 %collective-permute-start.9 = (bf16[128,1536]{1,0:T(8,128)(2,1)S(1)}, bf16[128,1536]{1,0:T(8,128)(2,1)S(1)}, u32[]{:S(2)}, u32[]{:S(2)}) collective-permute-start(bf16[128,1536]{1,0:T(8,128)(2,1)S(1)} %get-tuple-element.58), channel_id=1, source_target_pairs={{0,16},{8,24},{16,0},{24,8},{2,18},{10,26},{18,2},{26,10},{4,20},{... | collective-permute-start | bytes 1179656 | tf_op jit(solution)/shard_map/hidden_exchange/ppermute | solution.py:64
  45.5 20.4 %collective-permute-start.10 = (bf16[128,1536]{1,0:T(8,128)(2,1)S(1)}, bf16[128,1536]{1,0:T(8,128)(2,1)S(1)}, u32[]{:S(2)}, u32[]{:S(2)}) collective-permute-start(bf16[128,1536]{1,0:T(8,128)(2,1)S(1)} %get-tuple-element.59), channel_id=1, source_target_pairs={{0,24},{8,16},{16,8},{24,0},{2,26},{10,18},{18,10},{26,2},{4,28},{... | collective-permute-start | bytes 1179656 | tf_op jit(solution)/shard_map/hidden_exchange/ppermute | solution.py:64
  47.9 18.0 %collective-permute-start.6 = (bf16[128,1024]{1,0:T(8,128)(2,1)S(1)}, bf16[128,1024]{1,0:T(8,128)(2,1)S(1)}, u32[]{:S(2)}, u32[]{:S(2)}) collective-permute-start(bf16[128,1024]{1,0:T(8,128)(2,1)S(1)} %get-tuple-element.53), channel_id=1, source_target_pairs={{0,4},{1,5},{2,6},{3,7},{4,0},{5,1},{6,2},{7,3},{8,12},{9,13},{10,... | collective-permute-start | bytes 786440 | tf_op jit(solution)/shard_map/shared_exchange/ppermute | solution.py:57
  51.2 14.7 %collective-permute-start.7 = (bf16[128,1024]{1,0:T(8,128)(2,1)S(1)}, bf16[128,1024]{1,0:T(8,128)(2,1)S(1)}, u32[]{:S(2)}, u32[]{:S(2)}) collective-permute-start(bf16[128,1024]{1,0:T(8,128)(2,1)S(1)} %get-tuple-element.54), channel_id=1, source_target_pairs={{0,6},{1,7},{2,4},{3,5},{4,2},{5,3},{6,0},{7,1},{8,14},{9,15},{10,... | collective-permute-start | bytes 786440 | tf_op jit(solution)/shard_map/shared_exchange/ppermute | solution.py:57
  77.9 14.5 %collective-permute-start.14 = (bf16[128,512]{1,0:T(8,128)(2,1)S(1)}, bf16[128,512]{1,0:T(8,128)(2,1)S(1)}, u32[]{:S(2)}, u32[]{:S(2)}) collective-permute-start(bf16[128,512]{1,0:T(8,128)(2,1)S(1)} %get-tuple-element.62), channel_id=1, source_target_pairs={{1,0},{3,2},{5,4},{7,6},{9,8},{11,10},{13,12},{15,14},{17,16},{19,... | collective-permute-start | bytes 393224 | tf_op jit(solution)/shard_map/down_exchange/ppermute | solution.py:96
  79.2 15.9 %collective-permute-start.15 = (bf16[128,512]{1,0:T(8,128)(2,1)S(1)}, bf16[128,512]{1,0:T(8,128)(2,1)S(1)}, u32[]{:S(2)}, u32[]{:S(2)}) collective-permute-start(bf16[128,512]{1,0:T(8,128)(2,1)S(1)} %get-tuple-element.63), channel_id=1, source_target_pairs={{1,2},{3,0},{5,6},{7,4},{9,10},{11,8},{13,14},{15,12},{17,18},{19,... | collective-permute-start | bytes 393224 | tf_op jit(solution)/shard_map/down_exchange/ppermute | solution.py:91
  80.5 18.4 %collective-permute-start.16 = (bf16[128,512]{1,0:T(8,128)(2,1)S(1)}, bf16[128,512]{1,0:T(8,128)(2,1)S(1)}, u32[]{:S(2)}, u32[]{:S(2)}) collective-permute-start(bf16[128,512]{1,0:T(8,128)(2,1)S(1)} %get-tuple-element.64), channel_id=1, source_target_pairs={{1,4},{3,6},{5,0},{7,2},{9,12},{11,14},{13,8},{15,10},{17,20},{19,... | collective-permute-start | bytes 393224 | tf_op jit(solution)/shard_map/down_exchange/ppermute | solution.py:91
  81.8 20.3 %collective-permute-start.17 = (bf16[128,512]{1,0:T(8,128)(2,1)S(1)}, bf16[128,512]{1,0:T(8,128)(2,1)S(1)}, u32[]{:S(2)}, u32[]{:S(2)}) collective-permute-start(bf16[128,512]{1,0:T(8,128)(2,1)S(1)} %get-tuple-element.65), channel_id=1, source_target_pairs={{1,6},{3,4},{5,2},{7,0},{9,14},{11,12},{13,10},{15,8},{17,22},{19,... | collective-permute-start | bytes 393224 | tf_op jit(solution)/shard_map/down_exchange/ppermute | solution.py:91
  104.8 15.9 %collective-permute-start.19 = (bf16[128,1024]{1,0:T(8,128)(2,1)S(1)}, bf16[128,1024]{1,0:T(8,128)(2,1)S(1)}, u32[]{:S(2)}, u32[]{:S(2)}) collective-permute-start(bf16[128,1024]{1,0:T(8,128)(2,1)S(1)} %get-tuple-element.66.refs_1_.refs_8_), channel_id=1, source_target_pairs={{0,4},{2,6},{4,0},{6,2},{8,12},{10,14},{12,8},{14,10},{16,20},{18,... | collective-permute-start | bytes 786440 | tf_op jit(solution)/shard_map/st_zero_exchange/ppermute | solution.py:57
  122.3 14.8 %collective-permute-start.21 = (bf16[128,3584]{1,0:T(8,128)(2,1)S(1)}, bf16[128,3584]{1,0:T(8,128)(2,1)S(1)}, u32[]{:S(2)}, u32[]{:S(2)}) collective-permute-start(bf16[128,3584]{1,0:T(8,128)(2,1)S(1)} %get-tuple-element.70), channel_id=1, source_target_pairs={{1,9},{9,1},{17,25},{25,17},{3,11},{11,3},{19,27},{27,19},{5,13},{... | collective-permute-start | bytes 2752520 | tf_op jit(solution)/shard_map/dp_one_exchange/ppermute | solution.py:64
  123.0 16.5 %collective-permute-start.22 = (bf16[128,3584]{1,0:T(8,128)(2,1)S(1)}, bf16[128,3584]{1,0:T(8,128)(2,1)S(1)}, u32[]{:S(2)}, u32[]{:S(2)}) collective-permute-start(bf16[128,3584]{1,0:T(8,128)(2,1)S(1)} %get-tuple-element.71), channel_id=1, source_target_pairs={{1,17},{9,25},{17,1},{25,9},{3,19},{11,27},{19,3},{27,11},{5,21},{... | collective-permute-start | bytes 2752520 | tf_op jit(solution)/shard_map/dp_one_exchange/ppermute | solution.py:64
  123.8 15.8 %collective-permute-start.23 = (bf16[128,3584]{1,0:T(8,128)(2,1)S(1)}, bf16[128,3584]{1,0:T(8,128)(2,1)S(1)}, u32[]{:S(2)}, u32[]{:S(2)}) collective-permute-start(bf16[128,3584]{1,0:T(8,128)(2,1)S(1)} %get-tuple-element.72), channel_id=1, source_target_pairs={{1,25},{9,17},{17,9},{25,1},{3,27},{11,19},{19,11},{27,3},{5,29},{... | collective-permute-start | bytes 2752520 | tf_op jit(solution)/shard_map/dp_one_exchange/ppermute | solution.py:64
  133.7 16.7 %collective-permute-start.26 = (bf16[128,2048]{1,0:T(8,128)(2,1)S(1)}, bf16[128,2048]{1,0:T(8,128)(2,1)S(1)}, u32[]{:S(2)}, u32[]{:S(2)}) collective-permute-start(bf16[128,2048]{1,0:T(8,128)(2,1)S(1)} %get-tuple-element.77), channel_id=1, source_target_pairs={{0,16},{8,24},{16,0},{24,8},{2,18},{10,26},{18,2},{26,10},{4,20},{... | collective-permute-start | bytes 1572872 | tf_op jit(solution)/shard_map/dp_zero_exchange/ppermute | solution.py:64
  140.1 19.5 %collective-permute-start.24 = (bf16[4,128,512]{2,1,0:T(8,128)(2,1)S(1)}, bf16[4,128,512]{2,1,0:T(8,128)(2,1)}, u32[]{:S(2)}, u32[]{:S(2)}) collective-permute-start(bf16[4,128,512]{2,1,0:T(8,128)(2,1)S(1)} %backward_one_rest.1.refs_6_), channel_id=1, source_target_pairs={{1,0},{3,2},{5,4},{7,6},{9,8},{11,10},{13,12},{15,14},{17,16},{19,... | collective-permute-start | bytes 1572872 | tf_op jit(solution)/shard_map/down_late_exchange/ppermute | solution.py:852
  157.0 14.2 %all-to-all-start = ((f32[32,1,128]{2,1,0:T(1,128)}), f32[32,1,128]{2,1,0:T(1,128)S(1)}, u32[]{:S(2)}, u32[]{:S(2)}) async-start(f32[32,1,128]{2,1,0:T(1,128)} %bitcast.9), calls=%async_computation | async-start | bytes 32768 | tf_op jit(solution)/shard_map/norm_exchange/all_to_all | solution.py:863
  171.9 23.9 %collective-permute-start.28 = (bf16[128,1024]{1,0:T(8,128)(2,1)S(1)}, bf16[128,1024]{1,0:T(8,128)(2,1)S(1)}, u32[]{:S(2)}, u32[]{:S(2)}) collective-permute-start(bf16[128,1024]{1,0:T(8,128)(2,1)S(1)} %get-tuple-element.81), channel_id=1, source_target_pairs={{0,2},{1,3},{2,0},{3,1},{4,6},{5,7},{6,4},{7,5},{8,10},{9,11},{10,... | collective-permute-start | bytes 786440 | tf_op jit(solution)/shard_map/input_exchange/ppermute | solution.py:57
  173.6 22.2 %collective-permute-start.29 = (bf16[128,1024]{1,0:T(8,128)(2,1)S(1)}, bf16[128,1024]{1,0:T(8,128)(2,1)S(1)}, u32[]{:S(2)}, u32[]{:S(2)}) collective-permute-start(bf16[128,1024]{1,0:T(8,128)(2,1)S(1)} %get-tuple-element.82), channel_id=1, source_target_pairs={{0,4},{1,5},{2,6},{3,7},{4,0},{5,1},{6,2},{7,3},{8,12},{9,13},{10,... | collective-permute-start | bytes 786440 | tf_op jit(solution)/shard_map/input_exchange/ppermute | solution.py:57
  176.2 19.6 %collective-permute-start.30 = (bf16[128,1024]{1,0:T(8,128)(2,1)S(1)}, bf16[128,1024]{1,0:T(8,128)(2,1)S(1)}, u32[]{:S(2)}, u32[]{:S(2)}) collective-permute-start(bf16[128,1024]{1,0:T(8,128)(2,1)S(1)} %get-tuple-element.83), channel_id=1, source_target_pairs={{0,6},{1,7},{2,4},{3,5},{4,2},{5,3},{6,0},{7,1},{8,14},{9,15},{10,... | collective-permute-start | bytes 786440 | tf_op jit(solution)/shard_map/input_exchange/ppermute | solution.py:57
  (34 other events, 466.8 us)

commit v2 on v1

--- a/solution.py
+++ b/solution.py
@@ -71,7 +71,9 @@
 
 
 def gather_tensor(x, layer):
-    return scatter_tensor([x] * lax.axis_size("tensor"), layer)
+    n = lax.axis_size("tensor")
+    got = {k: over_tensor(x, xor_pairs(n, k), layer) for k in reversed(far_first(n))}
+    return [x] + [got[k] for k in range(1, n)]
 
 
 def far_first(n):
@@ -181,28 +183,48 @@
 def prep_weights(lift_mask, proj_mask, lift, proj):
     steps = min(8, lift.shape[0] // BLK)
 
-    def body(lift_mask_ref, proj_mask_ref, lift_ref, proj_ref, lift_out, proj_out):
-        for mask, src, dst in (
-            (lift_mask_ref, lift_ref, lift_out),
-            (proj_mask_ref, proj_ref, proj_out),
-        ):
-            n_rows = src.shape[0] // BLK
-            for r in range(n_rows):
-                for c in range(src.shape[1] // BLK):
-                    at = (slice(r * BLK, (r + 1) * BLK), slice(c * BLK, (c + 1) * BLK))
-                    kept = mask[pl.program_id(0) * n_rows + r, c] > 0
-                    tile = src[at]
-                    dst[at] = jnp.where(kept, tile, jnp.zeros_like(tile))
-
-    specs = [
-        pl.BlockSpec((x.shape[0] // steps, x.shape[1]), lambda i: (i, 0)) for x in (lift, proj)
-    ]
+    def body(lift_mask_ref, proj_mask_ref, lift_h, proj_h, *refs):
+        lift_out, proj_out, lift_s, proj_s, lift_sem, proj_sem = refs
+        jobs = (
+            (lift_mask_ref, lift_h, lift_out, lift_s, lift_sem),
+            (proj_mask_ref, proj_h, proj_out, proj_s, proj_sem),
+        )
+        into = [loads(src, held, sem.at[0], steps) for _, src, _, held, sem in jobs]
+        back = [loads(held, dst, sem.at[1], steps) for _, _, dst, held, sem in jobs]
+        for i in range(steps):
+            for copies in into:
+                copies[i].start()
+        for i in range(steps):
+            for (mask, _, _, held, _), copies, stores in zip(jobs, into, back):
+                copies[i].wait()
+                n_rows = held.shape[0] // BLK // steps
+                for r in range(i * n_rows, (i + 1) * n_rows):
+                    for c in range(held.shape[1] // BLK):
+                        at = (slice(r * BLK, (r + 1) * BLK), slice(c * BLK, (c + 1) * BLK))
+
+                        @pl.when(mask[r, c] <= 0)
+                        def _(held=held, at=at):
+                            held[at] = jnp.zeros((BLK, BLK), BF)
+
+                stores[i].start()
+        for stores in back:
+            for copy in stores:
+                copy.wait()
+
     return pl.pallas_call(
         body,
-        grid=(steps,),
-        in_specs=[sspec(), sspec()] + specs,
-        out_specs=specs,
-        out_shape=[pltpu.HBM(lift.shape, BF), pltpu.HBM(proj.shape, BF)],
+        in_specs=[sspec(), sspec()] + [pl.BlockSpec(memory_space=pltpu.HBM)] * 2,
+        out_specs=[pl.BlockSpec(memory_space=pltpu.HBM)] * 2,
+        out_shape=[
+            pltpu.HBM(lift.shape, BF),
+            pltpu.HBM(proj.shape, BF),
+        ],
+        scratch_shapes=[
+            pltpu.VMEM(lift.shape, BF),
+            pltpu.VMEM(proj.shape, BF),
+            pltpu.SemaphoreType.DMA((2, steps)),
+            pltpu.SemaphoreType.DMA((2, steps)),
+        ],
         compiler_params=params(),
         name="prep_weights",
     )(lift_mask, proj_mask, in_hbm(lift), in_hbm(proj))
@@ -389,36 +411,40 @@
         st_s[n + (t ^ k)] = st_ref[k][:, hb:]
 
 
-def hidden_cotangent(st_s, slope_ref, proj_in, proj_ref, out_ref, n, hb, hid):
-    for cols in tiles_of(hid):
-        acc = None
-        for k in range(2 * n):
-            if cols.start == 0:
-                proj_in[k].wait()
-            part = dot_nn(st_s[k], proj_ref[k * hb : (k + 1) * hb, cols])
-            acc = part if acc is None else acc + part
-        out_ref[:, cols] = (acc * slope_ref[:, cols]).astype(BF)
-
-
-def mixed_part(pre, extra, shift_cot, lift_ref, part_s, n, hb):
+def hidden_cotangent(st_s, slope_ref, proj_in, proj_ref, acc_s, out_ref, n, hb, hid):
+    for k in range(2 * n):
+        proj_in[k].wait()
+        part = dot_nn(st_s[k], proj_ref[k * hb : (k + 1) * hb, :])
+        if k == 0:
+            acc_s[...] = part
+        elif k + 1 < 2 * n:
+            acc_s[...] += part
+        else:
+            out_ref[:, :hid] = ((acc_s[...] + part) * slope_ref[...]).astype(BF)
+
+
+def mixed_part(pre, extra, shift_cot, lift_in, lift_ref, part_s, n, hb):
     for b in range(n):
+        lift_in[b].wait()
         part = dot_nt(pre, lift_ref[b * hb : (b + 1) * hb, :])
         part_s[:, b * hb : (b + 1) * hb] = (part + extra(b)).astype(BF)
     part_s[:, n * hb :] = shift_cot
 
 
-def natural_columns(part_ref, inv_ref, hot_s, first, count, hb, store):
+def natural_columns(part_ref, inv_ref, hots, first, count, hb, store):
     width = part_ref.shape[1]
     span = span_of(width)
 
-    def one(q, _):
-        row = inv_ref[:, pl.ds(pl.multiple_of(q * hb, hb), hb)]
-        for i in range(0, width, span):
-            fill_hot(hot_s, i, row, float(i), span)
-        store(q, dot_nn(part_ref[...], hot_s[...]).astype(BF))
+    def two(i, _):
+        for j, hot_s in enumerate(hots):
+            q = first + 2 * i + j
+            row = inv_ref[:, pl.ds(pl.multiple_of(q * hb, hb), hb)]
+            for at in range(0, width, span):
+                fill_hot(hot_s, at, row, float(at), span)
+            store(q, dot_nn(part_ref[...], hot_s[...]).astype(BF))
         return 0
 
-    lax.fori_loop(first, first + count, one, 0)
+    lax.fori_loop(0, count // 2, two, 0)
 
 
 def backward_one(idx, st, ca, slope, inv, lift, proj, width, n):
@@ -431,25 +457,23 @@
         ca_ref, slope_ref, inv_ref, lift_h, proj_h = refs[n : n + 5]
         pre_ref, part_ref, nat_ref = refs[n + 5 : n + 8]
         second_out = refs[n + 8 : 2 * n + 8]
-        st_s, hot_s, lift_ref, proj_ref, lift_sem, proj_sem = refs[-6:]
+        st_s, acc_s, hot_a, hot_b, lift_ref, proj_ref, lift_sem, proj_sem = refs[-8:]
         t = idx_ref[0]
         proj_in = loads(proj_h, proj_ref, proj_sem, 2 * n)
         lift_in = loads(lift_h, lift_ref, lift_sem, n)
         for copy in proj_in + lift_in:
             copy.start()
         order_st(st_ref, st_s, t, n, hb)
-        hidden_cotangent(st_s, slope_ref, proj_in, proj_ref, pre_ref, n, hb, hid)
-        for copy in lift_in:
-            copy.wait()
+        hidden_cotangent(st_s, slope_ref, proj_in, proj_ref, acc_s, pre_ref, n, hb, hid)
         mixed_part(
             pre_ref[...], lambda b: jnp.where(t == b, ca_ref[...].astype(F32), 0.0),
-            st_ref[0][:, hb:], lift_ref, part_ref, n, hb,
+            st_ref[0][:, hb:], lift_in, lift_ref, part_ref, n, hb,
         )
 
         def store(q, block):
             nat_ref[q - n] = block
 
-        natural_columns(part_ref, inv_ref, hot_s, n, n, hb, store)
+        natural_columns(part_ref, inv_ref, (hot_a, hot_b), n, n, hb, store)
         for k in range(n):
             second_out[k][...] = nat_ref[t ^ k]
 
@@ -462,6 +486,8 @@
         [((rows, hid), BF), ((rows, width), BF), ((n, rows, hb), BF)] + [((rows, hb), BF)] * n,
         [
             pltpu.VMEM((2 * n, rows, hb), BF),
+            pltpu.VMEM((rows, hid), F32),
+            pltpu.VMEM((width, hb), BF),
             pltpu.VMEM((width, hb), BF),
             pltpu.VMEM(lift.shape, BF),
             pltpu.VMEM(proj.shape, BF),
@@ -508,39 +534,22 @@
     rows, width = part.shape
     hb = inv.shape[1] // (2 * n)
 
-    def body(idx_ref, part_ref, inv_ref, nat_ref, hot_s):
+    def body(idx_ref, part_ref, inv_ref, nat_ref, *hot):
         @pl.when(idx_ref[1] != 0)
         def _():
             def store(q, block):
                 nat_ref[q] = block
 
-            natural_columns(part_ref, inv_ref, hot_s, 0, n, hb, store)
+            natural_columns(part_ref, inv_ref, hot, 0, n, hb, store)
 
     return whole(
         body,
         "backward_one_rest",
         [(idx, pltpu.SMEM)] + on_vmem([part, inv]),
         [((n, rows, hb), BF)],
-        [pltpu.VMEM((width, hb), BF)],
+        [pltpu.VMEM((width, hb), BF)] * 2,
         deps=deps,
     )[0]
-
-
-def chunks_of(idx, stack, deps):
-    n, rows, cols = stack.shape[0] // 2, stack.shape[1], stack.shape[2]
-
-    def body(idx_ref, stack_ref, *out):
-        for k in range(n):
-            for i in range(2):
-                out[k][:, i * cols : (i + 1) * cols] = stack_ref[2 * (idx_ref[0] ^ k) + i]
-
-    return whole(
-        body,
-        "chunks_of",
-        [(idx, pltpu.SMEM)] + on_vmem([stack]),
-        [((rows, 2 * cols), BF)] * n,
-        deps=deps,
-    )
 
 
 def backward_zero(idx, st, slope, proj, n, n_dp, deps):
@@ -553,7 +562,7 @@
         st_ref = refs[:n]
         slope_ref, proj_h = refs[n : n + 2]
         pack = refs[n + 2 : n + 2 + n_dp]
-        st_s, proj_ref, proj_sem = refs[-3:]
+        st_s, acc_s, proj_ref, proj_sem = refs[-4:]
 
         @pl.when(idx_ref[1] == 0)
         def _():
@@ -561,7 +570,7 @@
             for copy in proj_in:
                 copy.start()
             order_st(st_ref, st_s, idx_ref[0], n, hb)
-            hidden_cotangent(st_s, slope_ref, proj_in, proj_ref, pack[0], n, hb, hid)
+            hidden_cotangent(st_s, slope_ref, proj_in, proj_ref, acc_s, pack[0], n, hb, hid)
             for j in range(1, n_dp):
                 pack[j][:, :hid] = pack[0][:, :hid]
             fill_pack(pack, st_s, idx_ref[2], n_dp, m, hid, hb)
@@ -573,6 +582,7 @@
         [((rows, hid + m * hb), BF)] * n_dp,
         [
             pltpu.VMEM((2 * n, rows, hb), BF),
+            pltpu.VMEM((rows, hid), F32),
             pltpu.VMEM(proj.shape, BF),
             pltpu.SemaphoreType.DMA((2 * n,)),
         ],
@@ -586,24 +596,24 @@
     hid = lift.shape[1]
 
     def body(idx_ref, st_ref, pack_ref, *refs):
-        got_ref, inv_ref, lift_h, low_ref, high_ref, nat_s, part_s, hot_s, lift_ref, lift_sem = refs
+        got_ref, inv_ref, lift_h, low_ref, high_ref = refs[:5]
+        out = refs[5 : 5 + n]
+        nat_s, part_s, hot_a, hot_b, lift_ref, lift_sem = refs[5 + n :]
 
         @pl.when(idx_ref[1] == 0)
         def _():
             lift_in = loads(lift_h, lift_ref, lift_sem, n)
             for copy in lift_in:
                 copy.start()
-            for copy in lift_in:
-                copy.wait()
             mixed_part(
-                pack_ref[:, :hid], lambda b: got_ref[b].astype(F32), st_ref[:, hb:], lift_ref,
-                part_s, n, hb,
+                pack_ref[:, :hid], lambda b: got_ref[b].astype(F32), st_ref[:, hb:], lift_in,
+                lift_ref, part_s, n, hb,
             )
 
             def store(q, block):
                 nat_s[q] = block
 
-            natural_columns(part_s, inv_ref, hot_s, 0, 2 * n, hb, store)
+            natural_columns(part_s, inv_ref, (hot_a, hot_b), 0, 2 * n, hb, store)
 
         @pl.when(idx_ref[1] != 0)
         def _():
@@ -611,6 +621,10 @@
                 nat_s[q] = low_ref[q]
                 nat_s[n + q] = high_ref[q]
 
+        for k in range(n):
+            for q in range(2):
+                out[k][:, q * hb : (q + 1) * hb] = nat_s[2 * (idx_ref[0] ^ k) + q]
+
     return whole(
         body,
         "natural_shares",
@@ -618,14 +632,16 @@
         + on_vmem([st_own, pack, low_one, inv])
         + [(lift, pltpu.HBM)]
         + on_vmem([low, high]),
-        [((2 * n, rows, hb), BF)],
+        [((rows, 2 * hb), BF)] * n,
         [
+            pltpu.VMEM((2 * n, rows, hb), BF),
             pltpu.VMEM((rows, width), BF),
+            pltpu.VMEM((width, hb), BF),
             pltpu.VMEM((width, hb), BF),
             pltpu.VMEM(lift.shape, BF),
             pltpu.SemaphoreType.DMA((n,)),
         ],
-    )[0]
+    )
 
 
 def fetch(idx_ref, kind, bund, zero, one, lhs, rhs, sem, wait):
@@ -675,22 +691,22 @@
     ]
 
 
-def weight_squares(idx, lift_mask, proj_mask, bund, zero, one, logs, hid):
+def weight_squares(idx, lift_mask, proj_mask, bund, zero, one, logs_zero, logs_one, hid, deps):
     n_dp = len(zero)
     lift_s = factors("lift", bund, zero, hid)
     proj_s = factors("proj", bund, zero, hid)
 
-    def body(idx_ref, lift_mask_ref, proj_mask_ref, log_ref, *refs):
+    def body(idx_ref, lift_mask_ref, proj_mask_ref, log_zero_ref, log_one_ref, *refs):
         packs = [refs[i * n_dp : (i + 1) * n_dp] for i in range(3)]
         refs = refs[3 * n_dp :]
         sum_ref, sq_s = refs[:2]
         groups = (("proj", proj_mask_ref, refs[2:5]), ("lift", lift_mask_ref, refs[5:8]))
-        for wait in (False, True):
-            for kind, _, (lhs, rhs, sem) in groups:
-                fetch(idx_ref, kind, *packs, lhs, rhs, sem, wait)
+        for kind, _, (lhs, rhs, sem) in groups:
+            fetch(idx_ref, kind, *packs, lhs, rhs, sem, False)
         sq_s[...] = jnp.zeros_like(sq_s)
         d = idx_ref[2]
-        for kind, mask, (lhs, rhs, _) in groups:
+        for kind, mask, (lhs, rhs, sem) in groups:
+            fetch(idx_ref, kind, *packs, lhs, rhs, sem, True)
             n_rows = lhs.shape[1]
             first = d * (n_rows // BLK)
             tile = min(512, n_rows)
@@ -708,77 +724,135 @@
                     sq_s[...] += total
         lane = lax.broadcasted_iota(jnp.int32, sum_ref.shape, 1)
         square = jnp.sum(sq_s[...])
-        log_sum = jnp.sum(log_ref[...])
+        log_sum = jnp.sum(jnp.where(idx_ref[1] == 0, log_zero_ref[...], log_one_ref[...]))
         sum_ref[...] = jnp.where(lane == 0, square, jnp.where(lane == 1, log_sum, 0.0))
 
     n_all = lax.axis_size("dp") * lax.axis_size("tensor") * lax.axis_size("layers")
     return whole(
         body,
         "weight_squares",
-        [(idx, pltpu.SMEM), (lift_mask, pltpu.SMEM), (proj_mask, pltpu.SMEM), (logs, pltpu.VMEM)]
+        [(idx, pltpu.SMEM), (lift_mask, pltpu.SMEM), (proj_mask, pltpu.SMEM)]
+        + on_vmem([logs_zero, logs_one])
         + [(x, pltpu.HBM) for x in list(bund) + list(zero) + list(one)],
         [((n_all, BLK), F32)],
         [pltpu.VMEM((8, BLK), F32)] + proj_s + lift_s,
+        deps=deps,
     )[0]
 
 
-def adam(idx, sums, kind, mask, bund, zero, one, moment, square, hid, dep):
-    n_dp = len(zero)
-    n_rows, n_cols = moment.shape
-    tile = min(256, n_rows)
+def adam(idx, sums, masks, sources, moments, squares, hid, dep, log_count):
+    n_dp = len(sources[0])
+    n_cols = moments[0].shape[1]
+    tile = min(2 * BLK, *(x.shape[0] for x in moments))
+    counts = [x.shape[0] // tile for x in moments]
+    firsts = (0, counts[0])
+    steps = sum(counts)
+    kinds = ("proj", "lift")
+    n_layers = lax.axis_size("layers")
     inv_one = 1.0 / (1.0 - beta_one**ADAM_STEP)
     inv_two = 1.0 / (1.0 - beta_two**ADAM_STEP)
 
-    def body(idx_ref, mask_ref, sums_ref, dep_ref, *refs):
+    def body(idx_ref, proj_mask_ref, lift_mask_ref, sums_ref, dep_ref, *refs):
         packs = [refs[i * n_dp : (i + 1) * n_dp] for i in range(3)]
-        m_ref, v_ref, first_ref, second_ref, upd_ref, lhs, rhs, sem = refs[3 * n_dp :]
-        step = pl.program_id(0)
-
-        @pl.when(step == 0)
-        def _():
-            for wait in (False, True):
-                fetch(idx_ref, kind, *packs, lhs, rhs, sem, wait)
-
-        row = idx_ref[2] * (n_rows // BLK) + step * (tile // BLK)
+        refs = refs[3 * n_dp :]
+        states = (refs[0:2], refs[2:4])
+        outs = (refs[4:7], refs[7:10])
+        log_ref = refs[10]
+        scratch = (refs[11:14], refs[14:17])
+        held = refs[17:20]
+        load_sem, store_sem = refs[20:22]
+        masks_ref = (proj_mask_ref, lift_mask_ref)
+
+        def rows_of(i):
+            return pl.ds(pl.multiple_of(i * tile, tile), tile)
+
+        def load(which, i):
+            return [
+                pltpu.make_async_copy(
+                    states[which][j].at[rows_of(i)],
+                    held[j].at[rows_of(firsts[which] + i)],
+                    load_sem.at[j, firsts[which] + i],
+                )
+                for j in range(2)
+            ]
+
+        def store(which, i):
+            return [
+                pltpu.make_async_copy(
+                    held[j].at[rows_of(firsts[which] + i)],
+                    outs[which][j].at[rows_of(i)],
+                    store_sem.at[j, firsts[which] + i],
+                )
+                for j in range(3)
+            ]
+
+        for which, (kind, (lhs, rhs, sem)) in enumerate(zip(kinds, scratch)):
+            fetch(idx_ref, kind, *packs, lhs, rhs, sem, False)
+            for i in range(counts[which]):
+                for copy in load(which, i):
+                    copy.start()
         square_total = jnp.sum(sums_ref[:, 0:1], axis=0, keepdims=True)
         factor = jnp.minimum(1.0, CLIP / (jnp.sqrt(square_total) + 1e-06))
-        left = lhs[:, pl.ds(pl.multiple_of(step * tile, tile), tile)]
-        for cols in tiles_of(n_cols):
-            grad = dot_tn(left, rhs[:, cols])
-            for i in range(tile // BLK):
-                for j in range(grad.shape[1] // BLK):
-                    at = (
-                        slice(i * BLK, (i + 1) * BLK),
-                        slice(cols.start + j * BLK, cols.start + (j + 1) * BLK),
-                    )
-                    kept = mask_ref[row + i, cols.start // BLK + j] > 0
-                    g = grad[i * BLK : (i + 1) * BLK, j * BLK : (j + 1) * BLK] * factor
-                    old_m, old_v = m_ref[at], v_ref[at]
-                    new_m = jnp.where(kept, beta_one * old_m + (1.0 - beta_one) * g, old_m)
-                    new_v = jnp.where(kept, beta_two * old_v + (1.0 - beta_two) * g * g, old_v)
-                    spread = new_v * inv_two
-                    upd = (new_m * inv_one) / (spread * lax.rsqrt(spread) + adam_eps)
-                    first_ref[at] = new_m
-                    second_ref[at] = new_v
-                    upd_ref[at] = jnp.where(kept, upd, 0.0)
-
-    spec = pl.BlockSpec((tile, n_cols), lambda i: (i, 0))
+        place = lax.broadcasted_iota(jnp.int32, sums_ref.shape, 0) % n_layers
+        lane = lax.broadcasted_iota(jnp.int32, sums_ref.shape, 1)
+        own_log = (place == idx_ref[1]) & (lane == 1)
+        log_ref[0] = jnp.sum(jnp.where(own_log, sums_ref[...], 0.0)) / log_count
+        for which in range(2):
+            lhs, rhs, sem = scratch[which]
+            mask_ref = masks_ref[which]
+            fetch(idx_ref, kinds[which], *packs, lhs, rhs, sem, True)
+
+            def update(i, _, which=which, lhs=lhs, rhs=rhs, mask_ref=mask_ref):
+                for copy in load(which, i):
+                    copy.wait()
+                row = (idx_ref[2] * counts[which] + i) * (tile // BLK)
+                rows = rows_of(firsts[which] + i)
+                left = lhs[:, rows_of(i)]
+                for cols in tiles_of(n_cols):
+                    grad = dot_tn(left, rhs[:, cols])
+                    for r in range(tile // BLK):
+                        sub = pl.ds(pl.multiple_of(rows.start + r * BLK, BLK), BLK)
+                        for j in range(grad.shape[1] // BLK):
+                            first_col = cols.start + j * BLK
+                            at = (sub, slice(first_col, first_col + BLK))
+                            kept = mask_ref[row + r, first_col // BLK] > 0
+                            g = grad[r * BLK : (r + 1) * BLK, j * BLK : (j + 1) * BLK] * factor
+                            old_m, old_v = held[0][at], held[1][at]
+                            new_m = beta_one * old_m + (1.0 - beta_one) * g
+                            new_v = beta_two * old_v + (1.0 - beta_two) * g * g
+                            spread = new_v * inv_two
+                            upd = (new_m * inv_one) / (spread * lax.rsqrt(spread) + adam_eps)
+                            held[0][at] = jnp.where(kept, new_m, old_m)
+                            held[1][at] = jnp.where(kept, new_v, old_v)
+                            held[2][at] = jnp.where(kept, upd, 0.0)
+                for copy in store(which, i):
+                    copy.start()
+                return 0
+
+            lax.fori_loop(0, counts[which], update, 0)
+        for which in range(2):
+            for i in range(counts[which]):
+                for copy in store(which, i):
+                    copy.wait()
+
+    operands = [in_hbm(x) for group in sources for x in group]
+    states = [in_hbm(x) for pair in zip(moments, squares) for x in pair]
+    hbm = pl.BlockSpec(memory_space=pltpu.HBM)
     return pl.pallas_call(
         body,
-        grid=(n_rows // tile,),
-        in_specs=[sspec()] * 2
+        in_specs=[sspec()] * 3
         + [vspec()]
         + [pl.BlockSpec(memory_space=pl.ANY)]
-        + [pl.BlockSpec(memory_space=pltpu.HBM)] * (3 * n_dp)
-        + [spec] * 2,
-        out_specs=[spec] * 3,
-        out_shape=[pltpu.HBM(moment.shape, F32)] * 3,
-        scratch_shapes=factors(kind, bund, zero, hid),
-        compiler_params=pltpu.CompilerParams(vmem_limit_bytes=VMEM_LIMIT),
-        name="adam_" + kind,
-    )(
-        idx, mask, sums, dep, *map(in_hbm, (*bund, *zero, *one)), in_hbm(moment), in_hbm(square)
-    )
+        + [hbm] * (3 * n_dp + 4),
+        out_specs=[hbm] * 6 + [sspec()],
+        out_shape=[pltpu.HBM(x.shape, F32) for x in moments for _ in range(3)]
+        + [jax.ShapeDtypeStruct((1,), F32)],
+        scratch_shapes=[x for kind in kinds for x in factors(kind, sources[0], sources[1], hid)]
+        + [pltpu.VMEM((steps * tile, n_cols), F32)] * 3
+        + [pltpu.SemaphoreType.DMA((2, steps)), pltpu.SemaphoreType.DMA((3, steps))],
+        compiler_params=pltpu.CompilerParams(vmem_limit_bytes=28 * 1024 * 1024),
+        name="adam",
+    )(idx, *masks, sums, dep, *operands, *states)
 
 
 def total(parts):
@@ -822,8 +896,8 @@
     own = lax.dynamic_slice_in_dim(perm, half + t * hb, hb, 0)
     perm_cols = jnp.concatenate([perm[:half], own])[None].astype(F32)
     width = perm_cols.shape[1]
+    hid = lift_weight.shape[2]
     lift, proj = prep_weights(lift_mask, proj_mask, lift_weight[0], proj_weight[0])
-    hid = lift.shape[1]
 
     slope, columns, hidden, shared = forward(
         idx, tokens, perm_cols, lift, proj, n, (ca, cb)
@@ -834,49 +908,52 @@
         bund = scatter_dp(bundles(idx, columns, hidden, half, n_dp), 0)
     inv = prep_inverse(perm_cols, feat, (columns,))
 
-    st_own, logs = couple(shared, columns, half, [cb], (inv,) + tuple(bund[1:]))
+    st_own, logs_one = couple(shared, columns, half, [cb], (inv,) + tuple(bund[1:]))
     with jax.named_scope("st_one_exchange"):
         st = gather_tensor(st_own, 1)
     pre, part, high, second = backward_one(idx, st, ca, slope, inv, lift, proj, width, n)
     with jax.named_scope("down_exchange"):
         cb_zero = down_a_section(second)
 
-    st_own, _ = couple(shared, columns, half, cb_zero, ())
+    st_own, logs_zero = couple(shared, columns, half, cb_zero[::-1], ())
     with jax.named_scope("st_zero_exchange"):
         st_zero = gather_tensor(st_own, 0)
-    pack_one = packs_one(idx, st, pre, columns, hidden, half, n_dp, tuple(st_zero))
+    pack_zero = backward_zero(idx, st_zero, slope, proj, n, n_dp, ())
+    with jax.named_scope("dp_zero_exchange"):
+        pack_got = scatter_dp(pack_zero, 0)
+    pack_one = packs_one(idx, st, pre, columns, hidden, half, n_dp, (pack_zero[0],))
     with jax.named_scope("dp_one_exchange"):
         pack_one = scatter_dp(pack_one, 1)
     low = backward_one_rest(idx, part, inv, n, tuple(pack_one[1:]))
     with jax.named_scope("down_late_exchange"):
         low_one = lax.ppermute(low, "layers", [(1, 0)])
-    pack_zero = backward_zero(idx, st_zero, slope, proj, n, n_dp, ())
-    with jax.named_scope("dp_zero_exchange"):
-        pack_got = scatter_dp(pack_zero, 0)
     shares = natural_shares(
         idx, st_own, pack_zero[0], low_one, inv, lift, low, high, width, n
     )
 
-    sources = (bund, pack_got, pack_one)
-    sums = weight_squares(idx, lift_mask, proj_mask, *sources, logs, hid)
+    order = [0] + list(reversed(range(1, n_dp)))
+    sources = tuple([group[k] for k in order] for group in (bund, pack_got, pack_one))
+    sums = weight_squares(idx, lift_mask, proj_mask, *sources, logs_zero, logs_one, hid, tuple(shares))
     with jax.named_scope("norm_exchange"):
         sums = lax.all_to_all(
             sums, ("dp", "tensor", "layers"), split_axis=0, concat_axis=0, tiled=True
         )
-    shares = chunks_of(idx, shares, (sums,))
-    lift_out = adam(
-        idx, sums, "lift", lift_mask, *sources, lift_moment[0], lift_square[0], hid, shares[0]
-    )
     with jax.named_scope("input_exchange"):
-        shares = scatter_tensor(shares, None)
-    proj_out = adam(
-        idx, sums, "proj", proj_mask, *sources, proj_moment[0], proj_square[0], hid, shares[0]
-    )
-
-    input_grad = total(shares)[None]
-    by_section = sums.reshape(n_dp * n, -1, BLK)
-    log_total = jnp.sum(lax.dynamic_index_in_dim(by_section, section, 1, False)[:, 1])
-    log_det = (log_total / (rows * n_dp * half)).reshape(1)
+        got = scatter_tensor(shares, None)
+    updated = adam(
+        idx,
+        sums,
+        (proj_mask, lift_mask),
+        sources,
+        (proj_moment[0], lift_moment[0]),
+        (proj_square[0], lift_square[0]),
+        hid,
+        shares[0],
+        rows * n_dp * half,
+    )
+    proj_out, lift_out, log_det = updated[:3], updated[3:6], updated[6]
+
+    input_grad = total(got)[None]
     return (
         input_grad,
         log_det,

time: 199 us -> 181 us (0.910)
  Pallas kernels: 79.4 us -> 67.8 us
  blocking collectives: 0 us -> 10.8 us
  waiting for transfers between devices: 46.7 us -> 37.3 us
  local copies, waits for them, and re-layouts: 8.23 us -> 4.87 us
  starting transfers between devices: 57.8 us -> 55.4 us
    all_to_all x0 -> x1, blocking collectives: none -> 10.8 us  [per_device(): lax.all_to_all(sums, ('dp', 'tensor', 'layers'), split_axis=0, concat_axi...]
    ppermute x1, waiting for transfers between devices: 9.3 us -> 0.01 us  [down_a_section(): got[0] = lax.ppermute(chunks[0], 'layers', [(1, 0)])]
    ppermute x9, waiting for transfers between devices: 8.94 us -> 0.02 us  [over_dp(): return lax.ppermute(x, ('dp', 'layers'), route)]
    ppermute x3, waiting for transfers between devices: 9.71 us -> 17.4 us  [down_a_section(): lax.ppermute(chunks[k], ('tensor', 'layers'), [(i * m + 1, j * m) for i,...]
    pallas_call x3 -> x2, Pallas kernels: 30.7 us -> 23.3 us  [the longest x1 12.6 us: adam(): pl.pallas_call(body, in_specs=[sspec()] * 3 + [vspec()] + [pl.BlockSpec(m...]
    pallas_call x12 -> x11, Pallas kernels: 48.7 us -> 44.5 us  [whole(): pl.pallas_call(run, in_specs=specs + [pl.BlockSpec(memory_space=pl.ANY)]...]
    unnamed x53 -> x27, local copies, waits for them, and re-layouts: 6.07 us -> 2.73 us
    all_to_all x1 -> x0, starting transfers between devices: 2.56 us -> none  [per_device(): lax.all_to_all(sums, ('dp', 'tensor', 'layers'), split_axis=0, concat_axi...]
  transfers between devices with their start and end apart: 32 -> 31, of which waited for: 9 -> 6; matrix products, arithmetic and copies ran while one was open for 2% -> 2% of each run, Pallas kernels for 30% -> 24%
where the time goes in v2:
time: 181 us; the launch traced here: 179 us
  Pallas kernels  67.8 us (37%)
  starting transfers between devices  55.4 us (31%)
  waiting for transfers between devices  37.3 us (21%)
  blocking collectives  10.8 us (6%)
  local copies, waits for them, and re-layouts  4.87 us (3%)
  other arithmetic  2.05 us (1%)
    pallas_call x11, Pallas kernels, whole(): pl.pallas_call(run, in_specs=specs + [pl.BlockSpec(memory_space=pl.ANY)]...  44.5 us
    ppermute x17, starting transfers between devices, over_tensor(): return lax.ppermute(x, ('tensor', 'layers'), route)  28.4 us
    ppermute x9, starting transfers between devices, over_dp(): return lax.ppermute(x, ('dp', 'layers'), route)  20.6 us
    ppermute x17, waiting for transfers between devices, over_tensor(): return lax.ppermute(x, ('tensor', 'layers'), route)  19.8 us
    ppermute x3, waiting for transfers between devices, down_a_section(): lax.ppermute(chunks[k], ('tensor', 'layers'), [(i * m + 1, j * m) for i,...  17.4 us
    pallas_call x1, Pallas kernels, adam(): pl.pallas_call(body, in_specs=[sspec()] * 3 + [vspec()] + [pl.BlockSpec(m...  12.6 us
    all_to_all x1, blocking collectives, per_device(): lax.all_to_all(sums, ('dp', 'tensor', 'layers'), split_axis=0, concat_axi...  10.8 us
    pallas_call x1, Pallas kernels, prep_weights(): pl.pallas_call(body, in_specs=[sspec(), sspec()] + [pl.BlockSpec(memory_s...  10.7 us
  transfers between devices with their start and end apart: 31, of which 6 were waited for; matrix products, arithmetic and copies ran while one was open for 2% of the time, Pallas kernels for 24%

profile of v2, /device:TPU:0, one launch (start us, length us, event | category | flops | bytes accessed | tf_op | source)
XLA Modules:
  0.0 179.4 jit_solution(1411206172633816913)
XLA Ops:
  0.6 5.1 %collective-permute-start.2 = (bf16[128,1024]{1,0:T(8,128)(2,1)}, bf16[128,1024]{1,0:T(8,128)(2,1)S(1)}, u32[]{:S(2)}, u32[]{:S(2)}) collective-permute-start(bf16[128,1024]{1,0:T(8,128)(2,1)} %bitcast.24), channel_id=1, source_target_pairs={{0,6},{1,7},{2,4},{3,5},{4,2},{5,3},{6,0},{7,1},{8,14},{9,15},{10,... | collective-permute-start | bytes 786440 | tf_op jit(solution)/shard_map/tokens_exchange/ppermute | solution.py:57
  11.7 10.7 %prep_weights.1 = (bf16[2048,1024]{1,0:T(8,128)(2,1)}, bf16[4096,1024]{1,0:T(8,128)(2,1)}) custom-call(s32[16,8]{1,0:T(8,128)S(1)} %copy.24.lift_mask_ref.refs_1_, s32[32,8]{1,0:T(8,128)S(1)} %bitcast.28, bf16[2048,1024]{1,0:T(8,128)(2,1)} %bitcast.34, bf16[4096,1024]{1,0:T(8,128)(2,1)} %bitcast.33), custom_call_target="tpu_custom_call" | custom-call | tf_op jit(solution)/shard_map/prep_weights/pallas_call | solution.py:214
  22.5 6.8 %collective-permute-done.1.refs_3_ = bf16[128,1024]{1,0:T(8,128)(2,1)S(1)} collective-permute-done((bf16[128,1024]{1,0:T(8,128)(2,1)}, bf16[128,1024]{1,0:T(8,128)(2,1)S(1)}, u32[]{:S(2)}, u32[]{:S(2)}) %collective-permute-start.1) | collective-permute-done | bytes 262176 | tf_op jit(solution)/shard_map/tokens_exchange/ppermute | solution.py:57
  29.2 8.7 %forward.1 = (f32[128,1024]{1,0:T(8,128)S(1)}, bf16[128,2560]{1,0:T(8,128)(2,1)S(1)}, bf16[128,1024]{1,0:T(8,128)(2,1)S(1)}, bf16[128,1024]{1,0:T(8,128)(2,1)S(1...) custom-call(s32[3]{0:T(128)S(1)} %pad_add_fusion.refs_0_.idx_ref, ...), custom_call_target="tpu_custom_call" | custom-call | tf_op jit(solution)/shard_map/forward/pallas_call | solution.py:127
  38.7 3.4 %collective-permute-start.8 = (bf16[128,1536]{1,0:T(8,128)(2,1)S(1)}, bf16[128,1536]{1,0:T(8,128)(2,1)S(1)}, u32[]{:S(2)}, u32[]{:S(2)}) collective-permute-start(bf16[128,1536]{1,0:T(8,128)(2,1)S(1)} %get-tuple-element.59), channel_id=1, source_target_pairs={{0,8},{8,0},{16,24},{24,16},{2,10},{10,2},{18,26},{26,18},{4,12},{... | collective-permute-start | bytes 1179656 | tf_op jit(solution)/shard_map/hidden_exchange/ppermute | solution.py:64
  42.1 3.4 %collective-permute-start.9 = (bf16[128,1536]{1,0:T(8,128)(2,1)S(1)}, bf16[128,1536]{1,0:T(8,128)(2,1)S(1)}, u32[]{:S(2)}, u32[]{:S(2)}) collective-permute-start(bf16[128,1536]{1,0:T(8,128)(2,1)S(1)} %get-tuple-element.60), channel_id=1, source_target_pairs={{0,16},{8,24},{16,0},{24,8},{2,18},{10,26},{18,2},{26,10},{4,20},{... | collective-permute-start | bytes 1179656 | tf_op jit(solution)/shard_map/hidden_exchange/ppermute | solution.py:64
  45.6 2.4 %collective-permute-start.10 = (bf16[128,1536]{1,0:T(8,128)(2,1)S(1)}, bf16[128,1536]{1,0:T(8,128)(2,1)S(1)}, u32[]{:S(2)}, u32[]{:S(2)}) collective-permute-start(bf16[128,1536]{1,0:T(8,128)(2,1)S(1)} %get-tuple-element.61), channel_id=1, source_target_pairs={{0,24},{8,16},{16,8},{24,0},{2,26},{10,18},{18,10},{26,2},{4,28},{... | collective-permute-start | bytes 1179656 | tf_op jit(solution)/shard_map/hidden_exchange/ppermute | solution.py:64
  48.0 3.3 %collective-permute-start.6 = (bf16[128,1024]{1,0:T(8,128)(2,1)S(1)}, bf16[128,1024]{1,0:T(8,128)(2,1)S(1)}, u32[]{:S(2)}, u32[]{:S(2)}) collective-permute-start(bf16[128,1024]{1,0:T(8,128)(2,1)S(1)} %get-tuple-element.55), channel_id=1, source_target_pairs={{0,4},{1,5},{2,6},{3,7},{4,0},{5,1},{6,2},{7,3},{8,12},{9,13},{10,... | collective-permute-start | bytes 786440 | tf_op jit(solution)/shard_map/shared_exchange/ppermute | solution.py:57
  52.4 7.4 %prep_inverse.1.refs_6_.refs_7_.refs_2_.refs_4_ = f32[1,4096]{1,0:T(1,128)S(1)} custom-call(f32[1,2560]{1,0:T(1,128)S(1)} %add_convert_fusion.refs_5_.refs_0_, bf16[128,2560]{1,0:T(8,128)(2,1)S(1)} %get-tuple-element.57.refs_1_.refs_5_.refs_8_.refs_6_), custom_call_target="tpu_custom_call" | custom-call | tf_op jit(solution)/shard_map/prep_inverse/pallas_call | solution.py:127
  59.8 6.1 %collective-permute-done.6.refs_2_ = bf16[128,1024]{1,0:T(8,128)(2,1)S(1)} collective-permute-done((bf16[128,1024]{1,0:T(8,128)(2,1)S(1)}, bf16[128,1024]{1,0:T(8,128)(2,1)S(1)}, u32[]{:S(2)}, u32[]{:S(2)}) %collective-permute-start.6) | collective-permute-done | bytes 262176 | tf_op jit(solution)/shard_map/shared_exchange/ppermute | solution.py:57
  68.5 9.0 %backward_one.1 = (bf16[128,1024]{1,0:T(8,128)(2,1)S(1)}, bf16[128,2560]{1,0:T(8,128)(2,1)S(1)}, bf16[4,128,512]{2,1,0:T(8,128)(2,1)S(1)}, bf16[128,512]{1,0:T(8...) custom-call(s32[3]{0:T(128)S(1)} %pad_add_fusion.refs_0_.idx_ref, ...), custom_call_target="tpu_custom_call" | custom-call | tf_op jit(solution)/shard_map/backward_one/pallas_call | solution.py:127
  82.7 15.0 %collective-permute-done.14.refs_4_ = bf16[128,512]{1,0:T(8,128)(2,1)S(1)} collective-permute-done((bf16[128,512]{1,0:T(8,128)(2,1)S(1)}, bf16[128,512]{1,0:T(8,128)(2,1)S(1)}, u32[]{:S(2)}, u32[]{:S(2)}) %collective-permute-start.14) | collective-permute-done | bytes 131104 | tf_op jit(solution)/shard_map/down_exchange/ppermute | solution.py:93
  97.7 2.4 %collective-permute-done.15.refs_5_ = bf16[128,512]{1,0:T(8,128)(2,1)S(1)} collective-permute-done((bf16[128,512]{1,0:T(8,128)(2,1)S(1)}, bf16[128,512]{1,0:T(8,128)(2,1)S(1)}, u32[]{:S(2)}, u32[]{:S(2)}) %collective-permute-start.15) | collective-permute-done | bytes 131104 | tf_op jit(solution)/shard_map/down_exchange/ppermute | solution.py:93
  100.6 2.9 %collective-permute-start.20 = (bf16[128,1024]{1,0:T(8,128)(2,1)S(1)}, bf16[128,1024]{1,0:T(8,128)(2,1)S(1)}, u32[]{:S(2)}, u32[]{:S(2)}) collective-permute-start(bf16[128,1024]{1,0:T(8,128)(2,1)S(1)} %get-tuple-element.68.refs_1_), channel_id=1, source_target_pairs={{0,6},{2,4},{4,2},{6,0},{8,14},{10,12},{12,10},{14,8},{16,22},{18,... | collective-permute-start | bytes 786440 | tf_op jit(solution)/shard_map/st_zero_exchange/ppermute | solution.py:57
  105.5 5.4 %collective-permute-start.18 = (bf16[128,1024]{1,0:T(8,128)(2,1)S(1)}, bf16[128,1024]{1,0:T(8,128)(2,1)S(1)}, u32[]{:S(2)}, u32[]{:S(2)}) collective-permute-start(bf16[128,1024]{1,0:T(8,128)(2,1)S(1)} %get-tuple-element.68.refs_1_), channel_id=1, source_target_pairs={{0,2},{2,0},{4,6},{6,4},{8,10},{10,8},{12,14},{14,12},{16,18},{18,... | collective-permute-start | bytes 786440 | tf_op jit(solution)/shard_map/st_zero_exchange/ppermute | solution.py:57
  110.9 5.5 %collective-permute-done.19.refs_3_ = bf16[128,1024]{1,0:T(8,128)(2,1)S(1)} collective-permute-done((bf16[128,1024]{1,0:T(8,128)(2,1)S(1)}, bf16[128,1024]{1,0:T(8,128)(2,1)S(1)}, u32[]{:S(2)}, u32[]{:S(2)}) %collective-permute-start.19) | collective-permute-done | bytes 262176 | tf_op jit(solution)/shard_map/st_zero_exchange/ppermute | solution.py:57
  117.8 4.4 %backward_zero.1 = (bf16[128,2048]{1,0:T(8,128)(2,1)S(1)}, bf16[128,2048]{1,0:T(8,128)(2,1)S(1)}, bf16[128,2048]{1,0:T(8,128)(2,1)S(1)}, bf16[128,2048]{1,0:T(8,128)(2,1)S(1)}) custom-call(s32[3]{0:T(128)S(1)} %pad_add_fusion.refs_0_.idx_ref, bf16[128,1024]{1,0:T(8,128)(2,1)S(1)} %get-tuple-element.68.refs_1_, ...), custom_call_target="tpu_custom_call" | custom-call | tf_op jit(solution)/shard_map/backward_zero/pallas_call | solution.py:127
  127.8 4.4 %collective-permute-start.28 = (bf16[128,2048]{1,0:T(8,128)(2,1)S(1)}, bf16[128,2048]{1,0:T(8,128)(2,1)S(1)}, u32[]{:S(2)}, u32[]{:S(2)}) collective-permute-start(bf16[128,2048]{1,0:T(8,128)(2,1)S(1)} %get-tuple-element.83), channel_id=1, source_target_pairs={{0,24},{8,16},{16,8},{24,0},{2,26},{10,18},{18,10},{26,2},{4,28},{... | collective-permute-start | bytes 1572872 | tf_op jit(solution)/shard_map/dp_zero_exchange/ppermute | solution.py:64
  132.2 2.4 %collective-permute-start.29 = (bf16[128,2048]{1,0:T(8,128)(2,1)S(1)}, bf16[128,2048]{1,0:T(8,128)(2,1)S(1)}, u32[]{:S(2)}, u32[]{:S(2)}) collective-permute-start(bf16[128,2048]{1,0:T(8,128)(2,1)S(1)} %get-tuple-element.84), channel_id=1, source_target_pairs={{0,16},{8,24},{16,0},{24,8},{2,18},{10,26},{18,2},{26,10},{4,20},{... | collective-permute-start | bytes 1572872 | tf_op jit(solution)/shard_map/dp_zero_exchange/ppermute | solution.py:64
  134.6 2.5 %collective-permute-start.30 = (bf16[128,2048]{1,0:T(8,128)(2,1)S(1)}, bf16[128,2048]{1,0:T(8,128)(2,1)S(1)}, u32[]{:S(2)}, u32[]{:S(2)}) collective-permute-start(bf16[128,2048]{1,0:T(8,128)(2,1)S(1)} %get-tuple-element.85), channel_id=1, source_target_pairs={{0,8},{8,0},{16,24},{24,16},{2,10},{10,2},{18,26},{26,18},{4,12},{... | collective-permute-start | bytes 1572872 | tf_op jit(solution)/shard_map/dp_zero_exchange/ppermute | solution.py:64
  137.1 7.2 %natural_shares.1 = (bf16[128,1024]{1,0:T(8,128)(2,1)S(1)}, bf16[128,1024]{1,0:T(8,128)(2,1)S(1)}, bf16[128,1024]{1,0:T(8,128)(2,1)S(1)}, bf16[128,1024]{1,0:T(8,128)(2,1)S(1)}) custom-call(s32[3]{0:T(128)S(1)} %pad_add_fusion.refs_0_.idx_ref, bf16[128,1024]{1,0:T(8,128)(2,1)S(1)} %get-tuple-element.68.refs_1_, ...), custom_call_target="tpu_custom_call" | custom-call | tf_op jit(solution)/shard_map/natural_shares/pallas_call | solution.py:127
  149.8 5.2 %weight_squares.1 = f32[32,128]{1,0:T(8,128)S(1)} custom-call(s32[3]{0:T(128)S(1)} %pad_add_fusion.refs_0_.idx_ref, s32[16,8]{1,0:T(8,128)S(1)} %copy.24.lift_mask_ref.refs_1_, s32[32,8]{1,0:T(8,128)S(1)} %bitcast.29, f32[1,512]{1,0:T(1,128)S(1)} %get-tuple-element.80.refs_3_, f32[1,512]{1,0:T(1,128)S(1)} %get-tuple-element.81.refs_4_, ...), custom_call_target="tpu_custom_call" | custom-call | tf_op jit(solution)/shard_map/weight_squares/pallas_call | solution.py:127
  155.0 10.8 %all_to_all.11 = f32[32,1,128]{2,1,0:T(1,128)S(1)} all-to-all(f32[32,1,128]{2,1,0:T(1,128)S(1)} %bitcast.31), channel_id=1, replica_groups=mesh['dp'=4,'tensor'=4,'layers'=2] {'dp','tensor','layers'}, dimensions={0} | all-to-all | bytes 32768 | tf_op jit(solution)/shard_map/norm_exchange/all_to_all | solution.py:938
  165.8 12.6 %adam.1 = (f32[1024,1024]{1,0:T(8,128)}, f32[1024,1024]{1,0:T(8,128)}, f32[1024,1024]{1,0:T(8,128)}, f32[512,1024]{1,0:T(8,128)}, f32[512,1024]{1,0:T(8,128)}, /*index=5*/f32[512,1024]{1,0:T(8,128)}, f32[1]{0:T(128)}) custom-call(s32[3]{0:T(128)S(1)} %pad_add_fusion.refs_0_.idx_ref, s32[32,8]{1,0:T(8,128)S(1)} %bitcast.30, ...), custom_call_target="tpu_custom_call" | custom-call | tf_op jit(solution)/shard_map/adam/pallas_call | solution.py:841
  (87 shorter events, 31.2 us)
Async XLA Ops:
  0.6 21.8 %collective-permute-start.2 = (bf16[128,1024]{1,0:T(8,128)(2,1)}, bf16[128,1024]{1,0:T(8,128)(2,1)S(1)}, u32[]{:S(2)}, u32[]{:S(2)}) collective-permute-start(bf16[128,1024]{1,0:T(8,128)(2,1)} %bitcast.24), channel_id=1, source_target_pairs={{0,6},{1,7},{2,4},{3,5},{4,2},{5,3},{6,0},{7,1},{8,14},{9,15},{10,... | collective-permute-start | bytes 786440 | tf_op jit(solution)/shard_map/tokens_exchange/ppermute | solution.py:57
  5.7 23.5 %collective-permute-start.1 = (bf16[128,1024]{1,0:T(8,128)(2,1)}, bf16[128,1024]{1,0:T(8,128)(2,1)S(1)}, u32[]{:S(2)}, u32[]{:S(2)}) collective-permute-start(bf16[128,1024]{1,0:T(8,128)(2,1)} %bitcast.25), channel_id=1, source_target_pairs={{0,4},{1,5},{2,6},{3,7},{4,0},{5,1},{6,2},{7,3},{8,12},{9,13},{10,... | collective-permute-start | bytes 786440 | tf_op jit(solution)/shard_map/tokens_exchange/ppermute | solution.py:57
  5.8 23.5 %collective-permute-start = (bf16[128,1024]{1,0:T(8,128)(2,1)}, bf16[128,1024]{1,0:T(8,128)(2,1)S(1)}, u32[]{:S(2)}, u32[]{:S(2)}) collective-permute-start(bf16[128,1024]{1,0:T(8,128)(2,1)} %bitcast.26), channel_id=1, source_target_pairs={{0,2},{1,3},{2,0},{3,1},{4,6},{5,7},{6,4},{7,5},{8,10},{9,11},{10,... | collective-permute-start | bytes 786440 | tf_op jit(solution)/shard_map/tokens_exchange/ppermute | solution.py:57
  7.4 15.0 %collective-permute-start.4 = (bf16[128,512]{1,0:T(8,128)(2,1)S(1)}, bf16[128,512]{1,0:T(8,128)(2,1)S(1)}, u32[]{:S(2)}, u32[]{:S(2)}) collective-permute-start(bf16[128,512]{1,0:T(8,128)(2,1)S(1)} %get-tuple-element.96), channel_id=1, source_target_pairs={{1,3},{3,7},{5,1},{7,5},{9,11},{11,15},{13,9},{15,13},{17,19},{19,... | collective-permute-start | bytes 393224 | tf_op jit(solution)/shard_map/cotangent_exchange/ppermute | solution.py:57
  8.1 14.4 %collective-permute-start.3 = (bf16[128,512]{1,0:T(8,128)(2,1)S(1)}, bf16[128,512]{1,0:T(8,128)(2,1)S(1)}, u32[]{:S(2)}, u32[]{:S(2)}) collective-permute-start(bf16[128,512]{1,0:T(8,128)(2,1)S(1)} %get-tuple-element.97), channel_id=1, source_target_pairs={{1,1},{3,5},{5,3},{7,7},{9,9},{11,13},{13,11},{15,15},{17,17},{19,... | collective-permute-start | bytes 393224 | tf_op jit(solution)/shard_map/cotangent_exchange/ppermute | solution.py:57
  38.0 13.3 %collective-permute-start.5 = (bf16[128,1024]{1,0:T(8,128)(2,1)S(1)}, bf16[128,1024]{1,0:T(8,128)(2,1)S(1)}, u32[]{:S(2)}, u32[]{:S(2)}) collective-permute-start(bf16[128,1024]{1,0:T(8,128)(2,1)S(1)} %get-tuple-element.54), channel_id=1, source_target_pairs={{0,2},{1,3},{2,0},{3,1},{4,6},{5,7},{6,4},{7,5},{8,10},{9,11},{10,... | collective-permute-start | bytes 786440 | tf_op jit(solution)/shard_map/shared_exchange/ppermute | solution.py:57
  38.7 27.2 %collective-permute-start.8 = (bf16[128,1536]{1,0:T(8,128)(2,1)S(1)}, bf16[128,1536]{1,0:T(8,128)(2,1)S(1)}, u32[]{:S(2)}, u32[]{:S(2)}) collective-permute-start(bf16[128,1536]{1,0:T(8,128)(2,1)S(1)} %get-tuple-element.59), channel_id=1, source_target_pairs={{0,8},{8,0},{16,24},{24,16},{2,10},{10,2},{18,26},{26,18},{4,12},{... | collective-permute-start | bytes 1179656 | tf_op jit(solution)/shard_map/hidden_exchange/ppermute | solution.py:64
  42.1 23.8 %collective-permute-start.9 = (bf16[128,1536]{1,0:T(8,128)(2,1)S(1)}, bf16[128,1536]{1,0:T(8,128)(2,1)S(1)}, u32[]{:S(2)}, u32[]{:S(2)}) collective-permute-start(bf16[128,1536]{1,0:T(8,128)(2,1)S(1)} %get-tuple-element.60), channel_id=1, source_target_pairs={{0,16},{8,24},{16,0},{24,8},{2,18},{10,26},{18,2},{26,10},{4,20},{... | collective-permute-start | bytes 1179656 | tf_op jit(solution)/shard_map/hidden_exchange/ppermute | solution.py:64
  45.6 20.4 %collective-permute-start.10 = (bf16[128,1536]{1,0:T(8,128)(2,1)S(1)}, bf16[128,1536]{1,0:T(8,128)(2,1)S(1)}, u32[]{:S(2)}, u32[]{:S(2)}) collective-permute-start(bf16[128,1536]{1,0:T(8,128)(2,1)S(1)} %get-tuple-element.61), channel_id=1, source_target_pairs={{0,24},{8,16},{16,8},{24,0},{2,26},{10,18},{18,10},{26,2},{4,28},{... | collective-permute-start | bytes 1179656 | tf_op jit(solution)/shard_map/hidden_exchange/ppermute | solution.py:64
  48.0 18.0 %collective-permute-start.6 = (bf16[128,1024]{1,0:T(8,128)(2,1)S(1)}, bf16[128,1024]{1,0:T(8,128)(2,1)S(1)}, u32[]{:S(2)}, u32[]{:S(2)}) collective-permute-start(bf16[128,1024]{1,0:T(8,128)(2,1)S(1)} %get-tuple-element.55), channel_id=1, source_target_pairs={{0,4},{1,5},{2,6},{3,7},{4,0},{5,1},{6,2},{7,3},{8,12},{9,13},{10,... | collective-permute-start | bytes 786440 | tf_op jit(solution)/shard_map/shared_exchange/ppermute | solution.py:57
  51.2 14.7 %collective-permute-start.7 = (bf16[128,1024]{1,0:T(8,128)(2,1)S(1)}, bf16[128,1024]{1,0:T(8,128)(2,1)S(1)}, u32[]{:S(2)}, u32[]{:S(2)}) collective-permute-start(bf16[128,1024]{1,0:T(8,128)(2,1)S(1)} %get-tuple-element.56), channel_id=1, source_target_pairs={{0,6},{1,7},{2,4},{3,5},{4,2},{5,3},{6,0},{7,1},{8,14},{9,15},{10,... | collective-permute-start | bytes 786440 | tf_op jit(solution)/shard_map/shared_exchange/ppermute | solution.py:57
  77.5 20.2 %collective-permute-start.14 = (bf16[128,512]{1,0:T(8,128)(2,1)S(1)}, bf16[128,512]{1,0:T(8,128)(2,1)S(1)}, u32[]{:S(2)}, u32[]{:S(2)}) collective-permute-start(bf16[128,512]{1,0:T(8,128)(2,1)S(1)} %get-tuple-element.64), channel_id=1, source_target_pairs={{1,6},{3,4},{5,2},{7,0},{9,14},{11,12},{13,10},{15,8},{17,22},{19,... | collective-permute-start | bytes 393224 | tf_op jit(solution)/shard_map/down_exchange/ppermute | solution.py:93
  78.8 21.3 %collective-permute-start.15 = (bf16[128,512]{1,0:T(8,128)(2,1)S(1)}, bf16[128,512]{1,0:T(8,128)(2,1)S(1)}, u32[]{:S(2)}, u32[]{:S(2)}) collective-permute-start(bf16[128,512]{1,0:T(8,128)(2,1)S(1)} %get-tuple-element.65), channel_id=1, source_target_pairs={{1,4},{3,6},{5,0},{7,2},{9,12},{11,14},{13,8},{15,10},{17,20},{19,... | collective-permute-start | bytes 393224 | tf_op jit(solution)/shard_map/down_exchange/ppermute | solution.py:93
  80.1 20.0 %collective-permute-start.16 = (bf16[128,512]{1,0:T(8,128)(2,1)S(1)}, bf16[128,512]{1,0:T(8,128)(2,1)S(1)}, u32[]{:S(2)}, u32[]{:S(2)}) collective-permute-start(bf16[128,512]{1,0:T(8,128)(2,1)S(1)} %get-tuple-element.66), channel_id=1, source_target_pairs={{1,2},{3,0},{5,6},{7,4},{9,10},{11,8},{13,14},{15,12},{17,18},{19,... | collective-permute-start | bytes 393224 | tf_op jit(solution)/shard_map/down_exchange/ppermute | solution.py:93
  81.4 18.7 %collective-permute-start.17 = (bf16[128,512]{1,0:T(8,128)(2,1)S(1)}, bf16[128,512]{1,0:T(8,128)(2,1)S(1)}, u32[]{:S(2)}, u32[]{:S(2)}) collective-permute-start(bf16[128,512]{1,0:T(8,128)(2,1)S(1)} %get-tuple-element.67), channel_id=1, source_target_pairs={{1,0},{3,2},{5,4},{7,6},{9,8},{11,10},{13,12},{15,14},{17,16},{19,... | collective-permute-start | bytes 393224 | tf_op jit(solution)/shard_map/down_exchange/ppermute | solution.py:98
  103.5 12.9 %collective-permute-start.19 = (bf16[128,1024]{1,0:T(8,128)(2,1)S(1)}, bf16[128,1024]{1,0:T(8,128)(2,1)S(1)}, u32[]{:S(2)}, u32[]{:S(2)}) collective-permute-start(bf16[128,1024]{1,0:T(8,128)(2,1)S(1)} %get-tuple-element.68.refs_1_), channel_id=1, source_target_pairs={{0,4},{2,6},{4,0},{6,2},{8,12},{10,14},{12,8},{14,10},{16,20},{18,... | collective-permute-start | bytes 786440 | tf_op jit(solution)/shard_map/st_zero_exchange/ppermute | solution.py:57
  105.5 12.3 %collective-permute-start.18 = (bf16[128,1024]{1,0:T(8,128)(2,1)S(1)}, bf16[128,1024]{1,0:T(8,128)(2,1)S(1)}, u32[]{:S(2)}, u32[]{:S(2)}) collective-permute-start(bf16[128,1024]{1,0:T(8,128)(2,1)S(1)} %get-tuple-element.68.refs_1_), channel_id=1, source_target_pairs={{0,2},{2,0},{4,6},{6,4},{8,10},{10,8},{12,14},{14,12},{16,18},{18,... | collective-permute-start | bytes 786440 | tf_op jit(solution)/shard_map/st_zero_exchange/ppermute | solution.py:57
  126.5 10.5 %collective-permute-start.24 = (bf16[4,128,512]{2,1,0:T(8,128)(2,1)S(1)}, bf16[4,128,512]{2,1,0:T(8,128)(2,1)S(1)}, u32[]{:S(2)}, u32[]{:S(2)}) collective-permute-start(bf16[4,128,512]{2,1,0:T(8,128)(2,1)S(1)} %backward_one_rest.1.refs_6_), channel_id=1, source_target_pairs={{1,0},{3,2},{5,4},{7,6},{9,8},{11,10},{13,12},{15,14},{17,16},{19,... | collective-permute-start | bytes 1572872 | tf_op jit(solution)/shard_map/down_late_exchange/ppermute | solution.py:929
  127.8 18.7 %collective-permute-start.28 = (bf16[128,2048]{1,0:T(8,128)(2,1)S(1)}, bf16[128,2048]{1,0:T(8,128)(2,1)S(1)}, u32[]{:S(2)}, u32[]{:S(2)}) collective-permute-start(bf16[128,2048]{1,0:T(8,128)(2,1)S(1)} %get-tuple-element.83), channel_id=1, source_target_pairs={{0,24},{8,16},{16,8},{24,0},{2,26},{10,18},{18,10},{26,2},{4,28},{... | collective-permute-start | bytes 1572872 | tf_op jit(solution)/shard_map/dp_zero_exchange/ppermute | solution.py:64
  132.2 16.6 %collective-permute-start.29 = (bf16[128,2048]{1,0:T(8,128)(2,1)S(1)}, bf16[128,2048]{1,0:T(8,128)(2,1)S(1)}, u32[]{:S(2)}, u32[]{:S(2)}) collective-permute-start(bf16[128,2048]{1,0:T(8,128)(2,1)S(1)} %get-tuple-element.84), channel_id=1, source_target_pairs={{0,16},{8,24},{16,0},{24,8},{2,18},{10,26},{18,2},{26,10},{4,20},{... | collective-permute-start | bytes 1572872 | tf_op jit(solution)/shard_map/dp_zero_exchange/ppermute | solution.py:64
  134.6 14.2 %collective-permute-start.30 = (bf16[128,2048]{1,0:T(8,128)(2,1)S(1)}, bf16[128,2048]{1,0:T(8,128)(2,1)S(1)}, u32[]{:S(2)}, u32[]{:S(2)}) collective-permute-start(bf16[128,2048]{1,0:T(8,128)(2,1)S(1)} %get-tuple-element.85), channel_id=1, source_target_pairs={{0,8},{8,0},{16,24},{24,16},{2,10},{10,2},{18,26},{26,18},{4,12},{... | collective-permute-start | bytes 1572872 | tf_op jit(solution)/shard_map/dp_zero_exchange/ppermute | solution.py:64
  144.4 34.0 %collective-permute-start.25 = (bf16[128,1024]{1,0:T(8,128)(2,1)S(1)}, bf16[128,1024]{1,0:T(8,128)(2,1)S(1)}, u32[]{:S(2)}, u32[]{:S(2)}) collective-permute-start(bf16[128,1024]{1,0:T(8,128)(2,1)S(1)} %get-tuple-element.77.refs_18_), channel_id=1, source_target_pairs={{0,2},{1,3},{2,0},{3,1},{4,6},{5,7},{6,4},{7,5},{8,10},{9,11},{10,... | collective-permute-start | bytes 786440 | tf_op jit(solution)/shard_map/input_exchange/ppermute | solution.py:57
  144.4 34.0 %collective-permute-start.26 = (bf16[128,1024]{1,0:T(8,128)(2,1)S(1)}, bf16[128,1024]{1,0:T(8,128)(2,1)S(1)}, u32[]{:S(2)}, u32[]{:S(2)}) collective-permute-start(bf16[128,1024]{1,0:T(8,128)(2,1)S(1)} %get-tuple-element.78.refs_19_), channel_id=1, source_target_pairs={{0,4},{1,5},{2,6},{3,7},{4,0},{5,1},{6,2},{7,3},{8,12},{9,13},{10,... | collective-permute-start | bytes 786440 | tf_op jit(solution)/shard_map/input_exchange/ppermute | solution.py:57
  146.6 31.9 %collective-permute-start.27 = (bf16[128,1024]{1,0:T(8,128)(2,1)S(1)}, bf16[128,1024]{1,0:T(8,128)(2,1)S(1)}, u32[]{:S(2)}, u32[]{:S(2)}) collective-permute-start(bf16[128,1024]{1,0:T(8,128)(2,1)S(1)} %get-tuple-element.79.refs_20_), channel_id=1, source_target_pairs={{0,6},{1,7},{2,4},{3,5},{4,2},{5,3},{6,0},{7,1},{8,14},{9,15},{10,... | collective-permute-start | bytes 786440 | tf_op jit(solution)/shard_map/input_exchange/ppermute | solution.py:57
  (20 other events, 180.6 us)
